TPU v7x, 512 devices: a whole 4x8x8 slice. The times are simulated.
512 devices in a mesh: mode: 128 (over y, z, core), mer: 4 (over x).
Axes of the slice: x: 4, y: 8, z: 8, core: 2. Of those that a mesh axis runs over, the one named last changes fastest.
Arguments:
- mode_cost: int32 [512], replicated, may hold values from 105 to 420, as said below
- iface_index: int32 [128], replicated, may hold values from 0 to 255, as said below
- basis: float32 [4, 2, 1024, 128, 256], P(None, None, 'mode', 'mer'), as said below
- radial: float32 [2, 256, 256], replicated, as said below
- axial: float32 [2, 128, 32], P(None, 'mer'), as said below
- flow_coupling: float32 [4, 128, 256], P(None, 'mer'), may hold values from -8 to 8
- swirl: float32 [128, 256], P('mer'), may hold values from -6 to 6
- shift: float32 [2], replicated, may hold values from 0.2 to 0.8
Outputs:
- new_vector: float32 [2, 1024, 128, 256], P(None, 'mode', 'mer')
- coeffs: float32 [2, 4], replicated
- norm: float32 [], replicated
Inputs may be any that keep to these rules, and one draw needn't show every extreme that they name: `mode_cost`: every group has 2 to 8 modes and one group has exactly 8; within a group all costs are equal. `iface_index`: distinct and increasing; the first is 0 and the last is 255. `basis`: entries of order one to some tens. `radial`: each matrix has a unit diagonal plus entries of order 1 / sqrt(256). `axial`: each block has a unit diagonal plus entries of order 1 / sqrt(32).
All inputs are finite; a program needn't handle non-finite values.
Results may differ from a plain program's by a relative error of at most 0.000075.
Values sent between devices are 32-bit elements; how exact they have to be, the bound alone decides.
No kernel may reach another device: no remote copies, remote signals or barrier semaphores. Data moves between devices by JAX's collectives and lax.ppermute only.
A program may use at most 64 MiB of HBM per device.

v0:
```python
import jax
import jax.numpy as jnp
from jax import lax
from jax.sharding import PartitionSpec as P

QUOTA = 840


penalty = 1.0
schur_diag = 2.2
epsilon = 1e-06


def passed_along(block, axis, distance):
    devices = range(lax.axis_size(axis))
    route = [(i - distance, i) for i in devices if i - distance in devices]
    return lax.ppermute(block, axis, route)


def padded_2(shard, sides, width):
    for axis, dim in sides:
        size, length = (lax.axis_size(axis), shard.shape[dim])
        up = [(i, (i + 1) % size) for i in range(size - 1)]
        down = [(j, i) for i, j in up]
        last = lax.slice_in_dim(shard, length - width, length, axis=dim)
        leading = lax.slice_in_dim(shard, 0, width, axis=dim)
        before = lax.ppermute(last, axis, up)
        after = lax.ppermute(leading, axis, down)
        shard = jnp.concatenate([before, shard, after], axis=dim)
    return shard


def solve_interface(rhs):
    count = rhs.shape[0]
    places = jnp.arange(count)
    diagonal = jnp.full((count,), schur_diag, rhs.dtype)
    below = jnp.where(places > 0, -1.0, 0.0).astype(rhs.dtype)
    above = jnp.where(places < count - 1, -1.0, 0.0).astype(rhs.dtype)
    return lax.linalg.tridiagonal_solve(below, diagonal, above, rhs)


def body(mode_cost, iface_index, basis, radial, axial, flow_coupling, swirl, shift):
    highest = lax.Precision.HIGHEST
    my_group = lax.axis_index("mode")
    slots = basis.shape[2]
    points = basis.shape[3]
    width = basis.shape[4]
    krylov = basis.shape[0]
    modes = mode_cost.shape[0]
    prefix = jnp.cumsum(mode_cost) - mode_cost
    owner = prefix // QUOTA
    count = jnp.sum((owner == my_group).astype(jnp.int32))
    start = jnp.sum((owner < my_group).astype(jnp.int32))
    below_count = jnp.sum((owner == my_group - 1).astype(jnp.int32))
    places = jnp.arange(slots)
    active = (places < count).astype(jnp.float32)
    basis_live = basis * active[None, None, :, None, None]
    current = basis_live[krylov - 1]
    lower_all = passed_along(current, "mode", 1)
    upper_all = passed_along(current, "mode", -1)
    lower = lax.dynamic_slice_in_dim(lower_all, below_count - 2, 2, axis=1)
    upper = upper_all[:, :2]
    radial_term = jnp.einsum("csir,tr->csit", current, radial[0], precision=highest)
    axial_term = jnp.einsum("ij,csjr->csir", axial[0], current, precision=highest)
    padded = padded_2(current, (("mer", 2),), 1)
    link = jnp.zeros_like(current)
    link = link.at[:, :, 0].add(padded[:, :, 0])
    link = link.at[:, :, -1].add(padded[:, :, -1])
    image = radial_term + (axial_term + penalty * link)
    empty = jnp.zeros((2, 2, points, width), current.dtype)
    extended = jnp.concatenate([lower, current, empty], axis=1)
    extended = lax.dynamic_update_slice_in_dim(extended, upper, count + 2, axis=1)
    for which, offset in enumerate((-2, -1, 1, 2)):
        image = image + flow_coupling[which] * extended[:, 2 + offset : 2 + offset + slots]
    wave = (start + places).astype(jnp.float32) / modes
    rotation = wave[:, None, None] * swirl[None]
    image_re = image[0] - rotation * current[1]
    image_im = image[1] + rotation * current[0]
    shifted_re = image_re - (shift[0] * current[0] - shift[1] * current[1])
    shifted_im = image_im - (shift[0] * current[1] + shift[1] * current[0])
    shifted = jnp.stack([shifted_re, shifted_im])
    local = jnp.einsum("ij,csjr->csir", axial[1], shifted, precision=highest)
    local = jnp.einsum("csir,tr->csit", local, radial[1], precision=highest)
    select = (iface_index[None, :] == jnp.arange(width)[:, None]).astype(jnp.float32)
    top_trace = jnp.einsum("csr,rp->csp", local[:, :, -1], select, precision=highest)
    bottom_trace = jnp.einsum("csr,rp->csp", local[:, :, 0], select, precision=highest)
    traces = lax.all_gather(jnp.stack([top_trace, bottom_trace])[None], "mer", axis=0, tiled=True)
    jumps = traces[:-1, 0] - traces[1:, 1]
    subdomains = lax.axis_size("mer")
    solved = solve_interface(jumps.reshape(subdomains - 1, -1)).reshape(jumps.shape)
    zero_row = jnp.zeros((1,) + jumps.shape[1:], jumps.dtype)
    padded_g = jnp.concatenate([zero_row, solved, zero_row], axis=0)
    my_sub = lax.axis_index("mer")
    g_lower = lax.dynamic_index_in_dim(padded_g, my_sub, 0, keepdims=False)
    g_upper = lax.dynamic_index_in_dim(padded_g, my_sub + 1, 0, keepdims=False)
    position = jnp.arange(points).astype(jnp.float32) / (points - 1)
    correction = (1.0 - position)[None, None, :, None] * g_lower[:, :, None, :] - position[
        None, None, :, None
    ] * g_upper[:, :, None, :]
    result = local + jnp.einsum("csip,rp->csir", correction, select, precision=highest)
    result = result * active[None, :, None, None]
    dof = float(modes * points * subdomains * width)
    part_re = jnp.einsum("kcsir,csir->k", basis_live, result, precision=highest)
    part_im = jnp.einsum(
        "ksir,sir->k", basis_live[:, 0], result[1], precision=highest
    ) - jnp.einsum("ksir,sir->k", basis_live[:, 1], result[0], precision=highest)
    summed_re, summed_im = lax.psum((part_re, part_im), ("mode", "mer"))
    proj_re = summed_re / dof
    proj_im = summed_im / dof
    rest_re = (
        result[0]
        - jnp.einsum("k,ksir->sir", proj_re, basis_live[:, 0], precision=highest)
        + jnp.einsum("k,ksir->sir", proj_im, basis_live[:, 1], precision=highest)
    )
    rest_im = (
        result[1]
        - jnp.einsum("k,ksir->sir", proj_re, basis_live[:, 1], precision=highest)
        - jnp.einsum("k,ksir->sir", proj_im, basis_live[:, 0], precision=highest)
    )
    rest_re, rest_im = (rest_re, rest_im)
    squares = lax.psum(jnp.sum(rest_re * rest_re) + jnp.sum(rest_im * rest_im), ("mode", "mer"))
    norm = jnp.sqrt(squares / dof + epsilon)
    new_vector = jnp.stack([rest_re, rest_im]) / norm
    return (new_vector, jnp.stack([proj_re, proj_im]), norm)


def solution(mesh):
    in_specs = (
        P(),
        P(),
        P(None, None, "mode", "mer", None),
        P(),
        P(None, "mer", None),
        P(None, "mer", None),
        P("mer", None),
        P(),
    )
    out_specs = (P(None, "mode", "mer", None), P(), P())
    return jax.shard_map(body, mesh=mesh, in_specs=in_specs, out_specs=out_specs, check_vma=False)
```

profile of v0, /device:TPU:1, one launch (start us, length us, event | category | flops | bytes accessed | tf_op | source)
XLA Modules:
  0.0 287.7 jit_solution(5280361114235576659)
XLA Ops:
  0.6 1.0 reduce-window.9
  1.6 0.1 slice.200
  1.7 0.1 slice_reduce_fusion
  1.8 1.5 convert_reduce_fusion
  3.3 0.7 compare_convert_fusion
  4.0 2.0 broadcast_multiply_fusion
  6.1 0.8 slice_bitcast_fusion.2
  6.9 5.4 %collective-permute-start.2 = (f32[2,8,32,256]{3,2,1,0:T(8,128)}, f32[2,8,32,256]{3,2,1,0:T(8,128)}, u32[]{:S(2)}, u32[]{:S(2)}) collective-permute-start(f32[2,8,32,256]{3,2,1,0:T(8,128)} %slice_bitcast_fusion.2), channel_id=1, source_target_pairs={{0,4},{4,8},{8,12},{12,16},{16,20},{20,24},{24,28},{28,32},{32,36}... | collective-permute-start | bytes 1572872 | tf_op jit(solution)/shard_map/ppermute | solution.py:17
  12.3 5.5 %collective-permute-start.3 = (f32[2,8,32,256]{3,2,1,0:T(8,128)}, f32[2,8,32,256]{3,2,1,0:T(8,128)}, u32[]{:S(2)}, u32[]{:S(2)}) collective-permute-start(f32[2,8,32,256]{3,2,1,0:T(8,128)} %slice_bitcast_fusion.2), channel_id=1, source_target_pairs={{4,0},{8,4},{12,8},{16,12},{20,16},{24,20},{28,24},{32,28},{36,32}... | collective-permute-start | bytes 1572872 | tf_op jit(solution)/shard_map/ppermute | solution.py:17
  17.8 1.0 fusion.82
  18.8 1.3 collective-permute-start
  20.1 1.3 collective-permute-start.1
  21.4 1.4 fusion.33
  22.9 0.6 fusion.85
  23.4 0.7 fusion.84
  24.1 0.6 fusion.83
  24.7 1.2 slice_bitcast_fusion
  26.0 0.7 convert_multiply_fusion.1
  32.6 0.1 pad.15.clone
  32.7 0.9 scatter-add.6
  33.5 1.6 scatter-add.9
  35.2 1.0 constant_dynamic-slice_fusion
  36.2 0.0 copy-start.10
  36.2 1.2 maximum_maximum_fusion
  37.4 0.9 slice_dynamic-update-slice_fusion
  38.4 0.8 fusion.7
  39.1 1.3 fusion.28
  40.4 0.6 convolution_bitcast_fusion
  41.0 0.6 fusion.31
  41.7 0.2 convolution_bitcast_fusion.2
  41.9 0.2 convolution_bitcast_fusion.3
  42.0 9.4 %all-gather = f32[8,2,8,128]{3,2,1,0:T(8,128)S(1)} all-gather(f32[2,2,8,128]{3,2,1,0:T(8,128)S(1)} %pad_maximum_fusion), channel_id=2, replica_groups=mesh['mode'=128,'mer'=4] {'mer'}, dimensions={0}, use_global_device_ids=true | all-gather | bytes 81920 | tf_op jit(solution)/shard_map/all_gather | solution.py:87
  51.4 0.7 constant_dynamic-update-slice_fusion.3
  52.1 0.7 constant_dynamic-update-slice_fusion.2
  52.8 0.7 constant_dynamic-update-slice_fusion.1
  53.5 0.4 fusion.8
  54.0 9.4 %fusion.9 = f32[4]{0:T(128)S(1)} fusion(f32[4,2,8,32,256]{4,3,2,1,0:T(8,128)S(1)} %broadcast_multiply_fusion, f32[2,8,32,256,1]{3,2,1,0,4:T(8,128)S(1)} %bitcast.212), kind=kOutput, calls=%fused_computation.16 | convolution fusion | flops 6291456 | bytes 2621456 | tf_op jit(solution)/shard_map/kcsir,csir->k/dot_general | solution.py:103
  63.4 4.8 %convolution_bitcast_fusion.4 = f32[4]{0:T(128)S(1)} fusion(f32[4,8,32,256]{3,2,1,0:T(8,128)S(1)} %copy-done, f32[8,32,256,1]{2,1,0,3:T(8,128)S(1)} %get-tuple-element.43), kind=kOutput, calls=%fused_computation.14 | convolution fusion | flops 3145728 | bytes 1310736 | tf_op jit(solution)/shard_map/ksir,sir->k/dot_general | solution.py:106
  68.1 5.0 %fusion.12 = f32[4]{0:T(128)S(1)} fusion(f32[4]{0:T(128)S(1)} %convolution_bitcast_fusion.4, f32[4,8,32,256]{3,2,1,0:T(8,128)S(1)} %get-tuple-element.39, f32[8,32,256,1]{2,1,0,3:T(8,128)S(1)} %get-tuple-element.42), kind=kOutput, calls=%fused_computation.17 | convolution fusion | flops 3145732 | bytes 1310752 | tf_op jit(solution)/shard_map/ksir,sir->k/dot_general | solution.py:104
  73.1 106.3 %all-reduce.1 = (f32[4]{0:T(128)S(1)}, f32[4]{0:T(128)S(1)}) all-reduce(f32[4]{0:T(128)S(1)} %fusion.12, f32[4]{0:T(128)S(1)} %fusion.9), channel_id=1, replica_groups=mesh['mode'=128,'mer'=4] {'mode','mer'}, use_global_device_ids=true, to_apply=%region_6.7 | all-reduce | flops 8 | bytes 64 | tf_op jit(solution)/shard_map/psum | solution.py:107
  179.4 2.3 fusion.21
  181.8 2.3 fusion.15
  184.1 2.3 fusion.17
  186.5 2.3 fusion.19
  188.8 0.8 multiply_reduce_fusion
  190.9 93.6 %psum.23 = f32[]{:T(128)} all-reduce(f32[]{:T(128)S(6)} %add.118), channel_id=1, replica_groups=mesh['mode'=128,'mer'=4] {'mode','mer'}, use_global_device_ids=true, to_apply=%region_9.10 | all-reduce | flops 1 | bytes 8 | tf_op jit(solution)/shard_map/psum | solution.py:121
  285.2 0.6 pad_maximum_fusion.1
  285.7 0.8 maximum_divide_fusion
  (44 shorter events, 0.2 us)
Async XLA Ops:
  4.0 17.4 %copy-start.6 = (f32[2,256,256]{2,1,0:T(8,128)S(1)}, f32[2,256,256]{2,1,0:T(8,128)}, u32[]{:S(2)}) copy-start(f32[2,256,256]{2,1,0:T(8,128)} %param.15) | copy-start | bytes 1572868
  6.1 16.8 %copy-start.8 = (f32[4,32,256]{2,1,0:T(8,128)S(1)}, f32[4,32,256]{2,1,0:T(8,128)}, u32[]{:S(2)}) copy-start(f32[4,32,256]{2,1,0:T(8,128)} %param.17) | copy-start | bytes 393220
  6.1 16.8 %copy-start.11 = (f32[2]{0:T(128)S(1)}, f32[2]{0:T(128)}, u32[]{:S(2)}) copy-start(f32[2]{0:T(128)} %param.19) | copy-start | bytes 28
  6.9 28.2 %collective-permute-start.2 = (f32[2,8,32,256]{3,2,1,0:T(8,128)}, f32[2,8,32,256]{3,2,1,0:T(8,128)}, u32[]{:S(2)}, u32[]{:S(2)}) collective-permute-start(f32[2,8,32,256]{3,2,1,0:T(8,128)} %slice_bitcast_fusion.2), channel_id=1, source_target_pairs={{0,4},{4,8},{8,12},{12,16},{16,20},{20,24},{24,28},{28,32},{32,36}... | collective-permute-start | bytes 1572872 | tf_op jit(solution)/shard_map/ppermute | solution.py:17
  12.3 25.1 %collective-permute-start.3 = (f32[2,8,32,256]{3,2,1,0:T(8,128)}, f32[2,8,32,256]{3,2,1,0:T(8,128)}, u32[]{:S(2)}, u32[]{:S(2)}) collective-permute-start(f32[2,8,32,256]{3,2,1,0:T(8,128)} %slice_bitcast_fusion.2), channel_id=1, source_target_pairs={{4,0},{8,4},{12,8},{16,12},{20,16},{24,20},{28,24},{32,28},{36,32}... | collective-permute-start | bytes 1572872 | tf_op jit(solution)/shard_map/ppermute | solution.py:17
  18.8 13.9 %collective-permute-start = (f32[2,8,1,256]{3,2,1,0:T(1,128)S(1)}, f32[2,8,1,256]{3,2,1,0:T(1,128)S(1)}, u32[]{:S(2)}, u32[]{:S(2)}) collective-permute-start(f32[2,8,1,256]{3,2,1,0:T(1,128)S(1)} %get-tuple-element.47), channel_id=1, source_target_pairs={{0,1},{1,2},{2,3},{4,5},{5,6},{6,7},{8,9},{9,10},{10,11},{12,13},{... | collective-permute-start | bytes 49160 | tf_op jit(solution)/shard_map/ppermute | solution.py:27
  20.1 13.4 %collective-permute-start.1 = (f32[2,8,1,256]{3,2,1,0:T(1,128)S(1)}, f32[2,8,1,256]{3,2,1,0:T(1,128)S(1)}, u32[]{:S(2)}, u32[]{:S(2)}) collective-permute-start(f32[2,8,1,256]{3,2,1,0:T(1,128)S(1)} %get-tuple-element.46), channel_id=1, source_target_pairs={{1,0},{2,1},{3,2},{5,4},{6,5},{7,6},{9,8},{10,9},{11,10},{13,12},{... | collective-permute-start | bytes 49160 | tf_op jit(solution)/shard_map/ppermute | solution.py:28
  26.0 12.4 %copy-start.9 = (f32[2,32,32]{2,1,0:T(8,128)S(1)}, f32[2,32,32]{2,1,0:T(8,128)}, u32[]{:S(2)}) copy-start(f32[2,32,32]{2,1,0:T(8,128)} %param.16) | copy-start | bytes 24580
  35.2 3.2 %copy-start.4 = (f32[2,8,32,256]{3,2,1,0:T(8,128)S(1)}, f32[2,8,32,256]{3,2,1,0:T(8,128)}, u32[]{:S(2)}) copy-start(f32[2,8,32,256]{3,2,1,0:T(8,128)} %fusion.33) | copy-start | bytes 1572868
  35.2 3.2 %copy-start.5 = (f32[2,8,32,256]{3,2,1,0:T(8,128)S(1)}, f32[2,8,32,256]{3,2,1,0:T(8,128)}, u32[]{:S(2)}) copy-start(f32[2,8,32,256]{3,2,1,0:T(8,128)} %scatter-add.9) | copy-start | bytes 1572868
  36.2 2.9 %copy-start.10 = (f32[32,256]{1,0:T(8,128)S(1)}, f32[32,256]{1,0:T(8,128)}, u32[]{:S(2)}) copy-start(f32[32,256]{1,0:T(8,128)} %param.18) | copy-start | bytes 98308
  38.3 2.7 copy-start.7
  39.1 2.6 copy-start.12
  53.9 9.5 %copy-start.2 = (f32[2,8,32,256]{3,2,1,0:T(8,128)}, f32[2,8,32,256]{3,2,1,0:T(8,128)S(1)}, u32[]{:S(2)}) copy-start(f32[2,8,32,256]{3,2,1,0:T(8,128)S(1)} %fusion.8) | copy-start | bytes 1572868
  54.0 9.4 %copy-start = (f32[4,8,32,256]{3,2,1,0:T(8,128)S(1)}, f32[4,8,32,256]{3,2,1,0:T(8,128)}, u32[]{:S(2)}) copy-start(f32[4,8,32,256]{3,2,1,0:T(8,128)} %get-tuple-element.38) | copy-start | bytes 3145732
  68.1 113.7 %copy-start.1 = (f32[4,8,32,256]{3,2,1,0:T(8,128)S(1)}, f32[4,8,32,256]{3,2,1,0:T(8,128)}, u32[]{:S(2)}) copy-start(f32[4,8,32,256]{3,2,1,0:T(8,128)} %get-tuple-element.38) | copy-start | bytes 3145732
  181.8 7.1 %copy-start.3 = (f32[2,8,32,256]{3,2,1,0:T(8,128)S(1)}, f32[2,8,32,256]{3,2,1,0:T(8,128)}, u32[]{:S(2)}) copy-start(f32[2,8,32,256]{3,2,1,0:T(8,128)} %copy-done.2) | copy-start | bytes 1572868
where the time goes:
time: 288 us
  blocking collectives  209 us (73%)
  matrix products  32.5 us (11%)
  starting transfers between devices  13.4 us (5%)
  other arithmetic  12.6 us (4%)
  between operations  10.1 us (4%)
  local copies, waits for them, and re-layouts  9.78 us (3%)
    psum x1, blocking collectives, body(): summed_re, summed_im = lax.psum((part_re, part_im), ('mode', 'mer'))  106 us
    psum x1, blocking collectives, body(): lax.psum(jnp.sum(rest_re * rest_re) + jnp.sum(rest_im * rest_im), ('mode'...  93.6 us
    ppermute x2, starting transfers between devices, passed_along(): return lax.ppermute(block, axis, route)  10.8 us
    dot_general x1, matrix products, body(): part_re = jnp.einsum('kcsir,csir->k', basis_live, result, precision=highest)  9.39 us
    all_gather x1, blocking collectives, body(): lax.all_gather(jnp.stack([top_trace, bottom_trace])[None], 'mer', axis=0,...  9.36 us
  transfers between devices with their start and end apart: 4, of which 0 were waited for; matrix products, arithmetic and copies ran while one was open for 4% of the time, Pallas kernels for 0%

commit v1 on v0

v1 whole, which is shorter than its diff:
```python
import functools
import math

import jax
import jax.numpy as jnp
import numpy as np
from jax import lax
from jax.experimental import pallas as pl
from jax.experimental.pallas import tpu as pltpu
from jax.sharding import Mesh
from jax.sharding import PartitionSpec as P

QUOTA = 840
PENALTY = 1.0
SCHUR_DIAG = 2.2
EPSILON = 1e-06

VMEM = pl.BlockSpec(memory_space=pltpu.VMEM)
ANY = pl.BlockSpec(memory_space=pl.ANY)
SMEM = pl.BlockSpec(memory_space=pltpu.SMEM)
F32 = jnp.float32
BF16 = jnp.bfloat16
NT = (((1,), (1,)), ((), ()))
NN = (((1,), (0,)), ((), ()))


def split(x):
    high = x.astype(BF16)
    return high, (x - high.astype(F32)).astype(BF16)


def dot3(a, b, dims):
    def one(x, y):
        return lax.dot_general(x, y, dims, preferred_element_type=F32)

    return one(a[0], b[0]) + (one(a[0], b[1]) + one(a[1], b[0]))


def block_diagonal(block, copies):
    n = block.shape[0]
    size = n * copies
    rows = lax.broadcasted_iota(jnp.int32, (n, size), 0)
    cols = lax.broadcasted_iota(jnp.int32, (n, size), 1)
    spread = jnp.where(cols % n == rows, 1.0, 0.0).astype(BF16)
    on = (
        lax.broadcasted_iota(jnp.int32, (size, size), 0) // n
        == lax.broadcasted_iota(jnp.int32, (size, size), 1) // n
    )
    parts = []
    for part in split(block):
        tiled = lax.dot_general(part, spread, NN, preferred_element_type=F32)
        tiled = jnp.concatenate([tiled] * copies, axis=0)
        parts.append(jnp.where(on, tiled, 0.0).astype(BF16))
    return parts


def layout_kernel(group_of, krylov, cost_ref, basis_ref, info_ref, other_ref, pair_ref, sems):
    group = group_of()
    even = lax.rem(group, 2) == 0

    def copy(at, ref, which, part):
        return pltpu.make_async_copy(
            basis_ref.at[krylov - 1, part, pl.ds(at, 2)], ref.at[part], sems.at[which, part]
        )

    @pl.when(even)
    def _():
        for part in range(2):
            copy(0, other_ref, 0, part).start()

    @pl.when(jnp.logical_not(even))
    def _():
        for part in range(2):
            copy(0, pair_ref, 0, part).start()

    cost = cost_ref[...]
    rows, lanes = cost.shape
    lane = lax.broadcasted_iota(jnp.int32, cost.shape, 1)
    row = lax.broadcasted_iota(jnp.int32, cost.shape, 0)
    total = cost
    step = 1
    while step < lanes:
        total = total + jnp.where(lane >= step, pltpu.roll(total, step, 1), 0)
        step *= 2
    prefix = total - cost
    for i in range(rows - 1):
        prefix = prefix + jnp.where(row > i, total[i : i + 1, lanes - 1 :], 0)
    base = 2 * rows * lanes
    both = jnp.where(prefix < group * QUOTA, 1.0, 0.0)
    both = both + jnp.where(prefix < (group + 1) * QUOTA, float(base), 0.0)
    both = jnp.sum(both).astype(jnp.int32)
    start = lax.rem(both, base)
    count = lax.div(both, base) - start

    top = jnp.maximum(count - 2, 0)

    @pl.when(even)
    def _():
        for part in range(2):
            copy(top, pair_ref, 1, part).start()

    @pl.when(jnp.logical_not(even))
    def _():
        for part in range(2):
            copy(top, other_ref, 1, part).start()

    info_ref[0] = count
    info_ref[1] = start
    for which in range(2):
        for part in range(2):
            copy(0, pair_ref, which, part).wait()


def inner_kernel(
    modes,
    info_ref,
    iface_ref,
    shift_ref,
    basis_ref,
    radial_ref,
    axial_ref,
    flow_ref,
    swirl_ref,
    local_ref,
    ends_ref,
    block_ref,
    radial1_ref,
    gram_ref,
    mask_ref,
    high_ref,
    low_ref,
):
    krylov, _, slots, points, width = basis_ref.shape
    count = info_ref[0]
    start = info_ref[1]
    rows = slots * points
    last = krylov - 1

    pairs = [(i, j) for i in range(krylov) for j in range(i, krylov)]
    n_sums = sum(1 if i == j else 2 for i, j in pairs)

    def gram_step(slot, sums):
        sums = list(sums)
        for r in range(0, points, 8):
            for c in range(0, width, 128):
                q = [
                    [basis_ref[k, p, slot, r : r + 8, c : c + 128] for p in range(2)]
                    for k in range(krylov)
                ]
                at = 0
                for i, j in pairs:
                    sums[at] = sums[at] + (q[i][0] * q[j][0] + q[i][1] * q[j][1])
                    at += 1
                    if i != j:
                        sums[at] = sums[at] + (q[i][0] * q[j][1] - q[i][1] * q[j][0])
                        at += 1
        return tuple(sums)

    sums = lax.fori_loop(0, count, gram_step, tuple(jnp.zeros((8, 128), F32) for _ in range(n_sums)))
    lane = lax.broadcasted_iota(jnp.int32, (1, 128), 1)
    gram = jnp.zeros((1, 128), F32)
    for i, s in enumerate(sums):
        gram = gram + jnp.where(lane == 2 * krylov + 1 + i, jnp.sum(s, keepdims=True), 0.0)
    gram_ref[...] = gram

    column = lax.broadcasted_iota(jnp.int32, (1, width), 1)

    def mark(i, mask):
        return jnp.where(column == iface_ref[i], 1.0, mask)

    mask_ref[...] = lax.fori_loop(0, iface_ref.shape[0], mark, jnp.zeros((1, width), F32), unroll=8)

    first_block = block_diagonal(axial_ref[0], slots)
    second_block = block_diagonal(axial_ref[1], slots)
    block_ref[0] = second_block[0]
    block_ref[1] = second_block[1]
    radial1 = split(radial_ref[1])
    radial1_ref[0] = radial1[0]
    radial1_ref[1] = radial1[1]
    radial0 = split(radial_ref[0])


    def current(part, slot):
        return jnp.where(slot < count, basis_ref[last, part, slot], 0.0)

    for part in range(2):
        for slot in range(slots):
            high, low = split(current(part, slot))
            high_ref[part, slot * points : (slot + 1) * points] = high
            low_ref[part, slot * points : (slot + 1) * points] = low

    for part in range(2):
        v = (high_ref[part], low_ref[part])
        image = dot3(v, radial0, NT) + dot3(first_block, v, NN)
        local_ref[part] = image.reshape(slots, points, width)

    for which, point in enumerate((points - 1, 0)):
        picked = jnp.concatenate(
            [
                jnp.where(s < count, basis_ref[last, part, s, point : point + 1], 0.0)
                for part in range(2)
                for s in range(slots)
            ],
            axis=0,
        )
        ends_ref[which] = dot3(split(picked), radial1, NT)

    sigma_re = shift_ref[0]
    sigma_im = shift_ref[1]
    for slot in range(slots):
        wave = (start + slot).astype(F32) / modes
        rotation = wave * swirl_ref[...]
        turn = rotation - sigma_im
        v_re = current(0, slot)
        v_im = current(1, slot)
        new = [
            local_ref[0, slot] - turn * v_im - sigma_re * v_re,
            local_ref[1, slot] + turn * v_re - sigma_re * v_im,
        ]
        for which, offset in enumerate((-2, -1, 1, 2)):
            if 0 <= slot + offset < slots:
                for part in range(2):
                    new[part] = new[part] + flow_ref[which] * current(part, slot + offset)
        for part in range(2):
            high, low = split(jnp.where(slot < count, new[part], 0.0))
            high_ref[part, slot * points : (slot + 1) * points] = high
            low_ref[part, slot * points : (slot + 1) * points] = low

    for part in range(2):
        x = (high_ref[part], low_ref[part])
        x = split(dot3(second_block, x, NN))
        local_ref[part] = dot3(x, radial1, NT).reshape(slots, points, width)


def halo_kernel(
    group_of,
    modes,
    info_ref,
    other_ref,
    pair_ref,
    flow_ref,
    block_ref,
    radial1_ref,
    ends_ref,
    axial_ref,
    before_ref,
    local_ref,
    message_ref,
):
    _, slots, points, width = local_ref.shape
    local_ref[...] = before_ref[...]
    count = info_ref[0]
    end = count + info_ref[1]
    group = group_of()
    even = lax.rem(group, 2) == 0
    inputs = []
    for part in range(2):
        lower = [jnp.where(even, other_ref[part, i], pair_ref[part, i]) for i in range(2)]
        upper = [jnp.where(even, pair_ref[part, i], other_ref[part, i]) for i in range(2)]
        lower = [jnp.where(group > 0, x, 0.0) for x in lower]
        upper = [jnp.where(end + i < modes, x, 0.0) for i, x in enumerate(upper)]
        inputs += [
            jnp.where(count > 0, flow_ref[0] * lower[0] + flow_ref[1] * lower[1], 0.0),
            jnp.where(count > 1, flow_ref[0] * lower[1], 0.0),
            flow_ref[3] * upper[0],
            flow_ref[2] * upper[0] + flow_ref[3] * upper[1],
        ]
    x = split(jnp.concatenate(inputs, axis=0))
    x = split(dot3((block_ref[0], block_ref[1]), x, NN))
    x = dot3(x, (radial1_ref[0], radial1_ref[1]), NT).reshape(2, 4, points, width)
    for i, slot in enumerate((0, 1, jnp.maximum(count - 2, 0), jnp.maximum(count - 1, 0))):
        for part in range(2):
            local_ref[part, slot] = local_ref[part, slot] + x[part, i]
    wide = 2 * slots
    traces = [
        jnp.concatenate(
            [local_ref[part, s, point : point + 1] for part in range(2) for s in range(slots)], axis=0
        )
        for point in (points - 1, 0)
    ]
    corners = jnp.concatenate(
        [
            jnp.broadcast_to(axial_ref[1, i : i + 1, j : j + 1], (1, width))
            for i in (points - 1, 0)
            for j in (0, points - 1)
        ]
        + [jnp.zeros((4, width), F32)],
        axis=0,
    )
    for to in range(message_ref.shape[0]):
        message_ref[to, 0:wide] = traces[0]
        message_ref[to, wide : 2 * wide] = traces[1]
        message_ref[to, 2 * wide : 3 * wide] = ends_ref[0]
        message_ref[to, 3 * wide : 4 * wide] = ends_ref[1]
        message_ref[to, 4 * wide :] = corners


def project_kernel(
    sub_of,
    inverse,
    info_ref,
    received_ref,
    mask_ref,
    axial_ref,
    basis_ref,
    gram_ref,
    before_ref,
    w_ref,
    sums_ref,
    rows_ref,
):
    krylov, _, slots, points, width = basis_ref.shape
    subs = received_ref.shape[0]
    wide = 2 * slots
    count = info_ref[0]
    sub = sub_of()
    after = [received_ref[s, 2 * wide : 3 * wide] for s in range(subs)]
    before = [received_ref[s, 3 * wide : 4 * wide] for s in range(subs)]
    tops = []
    bottoms = []
    for s in range(subs):
        top = received_ref[s, 0:wide]
        bottom = received_ref[s, wide : 2 * wide]
        corner = received_ref[s, 4 * wide :]
        if s > 0:
            top = top + PENALTY * corner[0:1] * after[s - 1]
            bottom = bottom + PENALTY * corner[2:3] * after[s - 1]
        if s < subs - 1:
            top = top + PENALTY * corner[1:2] * before[s + 1]
            bottom = bottom + PENALTY * corner[3:4] * before[s + 1]
        tops.append(top)
        bottoms.append(bottom)
    jumps = [(tops[j - 1] - bottoms[j]) * mask_ref[...] for j in range(1, subs)]

    def solved(at):
        g = jnp.zeros((wide, width), F32)
        for j in range(subs - 1):
            weight = F32(0.0)
            for i in range(subs - 1):
                weight = jnp.where(at == i + 1, F32(inverse[i, j]), weight)
            g = g + weight * jumps[j]
        return g

    def spread(i, x):
        for row in range(wide):
            rows_ref[i, row] = jnp.broadcast_to(x[row : row + 1], (8, width))

    spread(0, solved(sub))
    spread(1, -solved(sub + 1))
    previous = jnp.zeros((wide, width), F32)
    following = jnp.zeros((wide, width), F32)
    for s in range(subs):
        previous = jnp.where(sub == s + 1, PENALTY * after[s], previous)
        following = jnp.where(sub == s - 1, PENALTY * before[s], following)
    spread(2, previous)
    spread(3, following)

    position = lax.broadcasted_iota(jnp.int32, (points, 128), 0).astype(F32) / (points - 1)
    weights = [
        1.0 - position,
        position,
        jnp.broadcast_to(axial_ref[1, :, 0:1], (points, 128)),
        jnp.broadcast_to(axial_ref[1, :, points - 1 : points], (points, 128)),
    ]

    def step(slot, sums):
        sums = list(sums)
        for c in range(0, width, 128):
            rows = [
                [rows_ref[i, part * slots + slot, :, c : c + 128] for i in range(4)]
                for part in range(2)
            ]
            for r in range(0, points, 8):
                w = []
                for part in range(2):
                    x = before_ref[part, slot, r : r + 8, c : c + 128]
                    for i in range(4):
                        x = x + weights[i][r : r + 8] * rows[part][i]
                    w_ref[part, slot, r : r + 8, c : c + 128] = x
                    w.append(x)
                for k in range(krylov):
                    q = [basis_ref[k, part, slot, r : r + 8, c : c + 128] for part in range(2)]
                    sums[2 * k] = sums[2 * k] + (q[0] * w[0] + q[1] * w[1])
                    sums[2 * k + 1] = sums[2 * k + 1] + (q[0] * w[1] - q[1] * w[0])
                sums[2 * krylov] = sums[2 * krylov] + (w[0] * w[0] + w[1] * w[1])
        return tuple(sums)

    sums = lax.fori_loop(
        0, count, step, tuple(jnp.zeros((8, 128), F32) for _ in range(2 * krylov + 1))
    )
    lane = lax.broadcasted_iota(jnp.int32, (1, 128), 1)
    out = gram_ref[...]
    for i, s in enumerate(sums):
        out = out + jnp.where(lane == i, jnp.sum(s, keepdims=True), 0.0)
    for to in range(sums_ref.shape[0]):
        sums_ref[to] = out


def finish_kernel(dof, info_ref, sums_ref, basis_ref, w_ref, out_ref, coeffs_ref, norm_ref):
    krylov, _, slots, points, width = basis_ref.shape
    count = info_ref[0]
    total = jnp.sum(sums_ref[...], axis=0) / dof

    def at(i):
        return total[:, i : i + 1]

    re = [at(2 * k) for k in range(krylov)]
    im = [at(2 * k + 1) for k in range(krylov)]
    squares = at(2 * krylov)
    place = 2 * krylov + 1
    for i in range(krylov):
        squares = squares - 2.0 * (re[i] * re[i] + im[i] * im[i])
        for j in range(i, krylov):
            if i == j:
                squares = squares + (re[i] * re[i] + im[i] * im[i]) * at(place)
                place += 1
            else:
                both = (re[i] * re[j] + im[i] * im[j]) * at(place)
                cross = (re[i] * im[j] - im[i] * re[j]) * at(place + 1)
                squares = squares + 2.0 * (both - cross)
                place += 2
    norm = jnp.sqrt(squares + EPSILON)
    norm_ref[...] = norm
    coeffs_ref[...] = jnp.concatenate(
        [jnp.concatenate(re, axis=1), jnp.concatenate(im, axis=1)], axis=0
    )
    scale = jnp.broadcast_to(1.0 / norm, (8, 128))
    re = [jnp.broadcast_to(x, (8, 128)) for x in re]
    im = [jnp.broadcast_to(x, (8, 128)) for x in im]

    def live(slot, carry):
        for r in range(0, points, 8):
            for c in range(0, width, 128):
                rest_re = w_ref[0, slot, r : r + 8, c : c + 128]
                rest_im = w_ref[1, slot, r : r + 8, c : c + 128]
                for k in range(krylov):
                    q = [basis_ref[k, part, slot, r : r + 8, c : c + 128] for part in range(2)]
                    rest_re = rest_re - (re[k] * q[0] - im[k] * q[1])
                    rest_im = rest_im - (re[k] * q[1] + im[k] * q[0])
                out_ref[0, slot, r : r + 8, c : c + 128] = rest_re * scale
                out_ref[1, slot, r : r + 8, c : c + 128] = rest_im * scale
        return carry

    def empty(slot, carry):
        for part in range(2):
            out_ref[part, slot] = jnp.zeros((points, width), F32)
        return carry

    lax.fori_loop(0, count, live, 0)
    lax.fori_loop(count, slots, empty, 0)


def params(mebibytes=24):
    return pltpu.CompilerParams(vmem_limit_bytes=mebibytes * 2**20)


def body(outer, inner, mode_cost, iface_index, basis, radial, axial, flow_coupling, swirl, shift):
    krylov, _, slots, points, width = basis.shape
    modes = mode_cost.shape[0]
    groups = outer * inner
    subs = lax.axis_size("mer")

    def group_of():
        return lax.axis_index("outer") * inner + lax.axis_index("inner")

    def sub_of():
        return lax.axis_index("mer")

    mode = ("outer", "inner")
    shape = jax.ShapeDtypeStruct
    info, to_other, to_pair = pl.pallas_call(
        functools.partial(layout_kernel, group_of, krylov),
        out_shape=(
            shape((2,), jnp.int32),
            shape((2, 2, points, width), F32),
            shape((2, 2, points, width), F32),
        ),
        in_specs=[VMEM, ANY],
        out_specs=(SMEM, VMEM, VMEM),
        scratch_shapes=[pltpu.SemaphoreType.DMA((2, 2))],
        compiler_params=params(52),
        cost_estimate=pl.CostEstimate(flops=10**10, bytes_accessed=2**18, transcendentals=0),
        name="layout",
    )(mode_cost.reshape(-1, math.gcd(modes, 128)), basis)
    other = [(i, i + 1) for i in range(1, groups - 1, 2)]
    other += [(j, i) for i, j in other]
    from_other = lax.ppermute(to_other, mode, other)
    from_pair = lax.ppermute(to_pair, mode, [(i, i ^ 1) for i in range(groups)])

    rows = slots * points
    local, ends, block, radial1, gram, mask = pl.pallas_call(
        functools.partial(inner_kernel, modes),
        out_shape=(
            shape((2, slots, points, width), F32),
            shape((2, 2 * slots, width), F32),
            shape((2, rows, rows), BF16),
            shape((2, width, width), BF16),
            shape((1, 128), F32),
            shape((1, width), F32),
        ),
        in_specs=[SMEM, SMEM, SMEM, VMEM, VMEM, VMEM, VMEM, VMEM],
        out_specs=(VMEM,) * 6,
        scratch_shapes=[pltpu.VMEM((2, rows, width), BF16)] * 2,
        compiler_params=params(),
        cost_estimate=pl.CostEstimate(flops=10**9, bytes_accessed=8 * 2**20, transcendentals=0),
        name="inner",
    )(info, iface_index, shift, basis, radial, axial, flow_coupling, swirl)

    wide = 2 * slots
    local, message = pl.pallas_call(
        functools.partial(halo_kernel, group_of, modes),
        out_shape=(
            shape(local.shape, F32),
            shape((subs, 4 * wide + 8, width), F32),
        ),
        in_specs=[SMEM] + [VMEM] * 8,
        out_specs=(VMEM, VMEM),
        compiler_params=params(),
        name="halo",
    )(info, from_other, from_pair, flow_coupling, block, radial1, ends, axial, local)
    received = lax.all_to_all(message, "mer", 0, 0)

    system = np.diag(np.full(subs - 1, SCHUR_DIAG)) - np.eye(subs - 1, k=1) - np.eye(subs - 1, k=-1)
    w, sums = pl.pallas_call(
        functools.partial(project_kernel, sub_of, np.linalg.inv(system)),
        out_shape=(shape(local.shape, F32), shape((inner, 1, 128), F32)),
        in_specs=[SMEM] + [VMEM] * 6,
        out_specs=(VMEM, VMEM),
        scratch_shapes=[pltpu.VMEM((4, wide, 8, width), F32)],
        compiler_params=params(),
        name="project",
    )(info, received, mask, axial, basis, gram, local)

    sums = lax.all_to_all(sums, "inner", 0, 0)
    sums = jnp.broadcast_to(jnp.sum(sums, axis=0, keepdims=True), (outer * subs, 1, 128))
    sums = lax.all_to_all(sums, ("outer", "mer"), 0, 0)

    new_vector, coeffs, norm = pl.pallas_call(
        functools.partial(finish_kernel, float(modes * points * subs * width)),
        out_shape=(shape(local.shape, F32), shape((2, krylov), F32), shape((1, 1), F32)),
        in_specs=[SMEM] + [VMEM] * 3,
        compiler_params=params(),
        name="finish",
    )(info, sums, basis, w)
    return new_vector, coeffs, norm.reshape(())


def solution(mesh):
    groups, subs = mesh.devices.shape
    inner = math.gcd(16, groups // 2)
    outer = groups // inner
    fine = Mesh(mesh.devices.reshape(outer, inner, subs), ("outer", "inner", "mer"))
    mode = ("outer", "inner")
    in_specs = (
        P(),
        P(),
        P(None, None, mode, "mer", None),
        P(),
        P(None, "mer", None),
        P(None, "mer", None),
        P("mer", None),
        P(),
    )
    out_specs = (P(None, mode, "mer", None), P(), P())
    return jax.shard_map(
        functools.partial(body, outer, inner),
        mesh=fine,
        in_specs=in_specs,
        out_specs=out_specs,
        check_vma=False,
    )
```

time: 288 us -> 62.9 us (0.22)
  blocking collectives: 209 us -> 42.2 us
  matrix products: 32.5 us -> 0 us
  other arithmetic: 12.6 us -> 0.03 us
  Pallas kernels: 0 us -> 9.48 us
  between operations: 10.1 us -> 0.78 us
  local copies, waits for them, and re-layouts: 9.78 us -> 0.72 us
  starting transfers between devices: 13.4 us -> 9.46 us
    psum x2 -> x0, blocking collectives: 200 us -> none  [the longest x1 106 us: body(): summed_re, summed_im = lax.psum((part_re, part_im), ('mode', 'mer'))]
    all_to_all x0 -> x3, blocking collectives: none -> 42.2 us  [the longest x1 16.5 us: body(): sums = lax.all_to_all(sums, 'inner', 0, 0)]
    dot_general x14 -> x0, matrix products: 32.5 us -> none  [the longest x1 9.39 us: body(): part_re = jnp.einsum('kcsir,csir->k', basis_live, result, precision=highest)]
    pallas_call x0 -> x5, Pallas kernels: none -> 9.48 us  [the longest x1 2.73 us: body(): pl.pallas_call(functools.partial(inner_kernel, modes), out_shape=(shape((...]
    all_gather x1 -> x0, blocking collectives: 9.36 us -> none  [body(): lax.all_gather(jnp.stack([top_trace, bottom_trace])[None], 'mer', axis=0,...]
    ppermute x4 -> x2, starting transfers between devices: 13.4 us -> 9.46 us  [the longest x1 5.4 us: body(): from_other = lax.ppermute(to_other, mode, other)]
    slice x5 -> x0, local copies, waits for them, and re-layouts: 2.89 us -> none  [the longest x2 1.31 us: solve_interface(): return lax.linalg.tridiagonal_solve(below, diagonal, above, rhs)]
  transfers between devices with their start and end apart: 4 -> 2, of which waited for: 0 -> 0; matrix products, arithmetic and copies ran while one was open for 4% -> 0% of each run, Pallas kernels for 0% -> 4%
where the time goes in v1:
time: 62.9 us; the launch traced here: 62.6 us
  blocking collectives  42.2 us (67%)
  Pallas kernels  9.48 us (15%)
  starting transfers between devices  9.46 us (15%)
  between operations  0.78 us (1%)
  local copies, waits for them, and re-layouts  0.72 us (1%)
    all_to_all x1, blocking collectives, body(): sums = lax.all_to_all(sums, 'inner', 0, 0)  16.5 us
    all_to_all x1, blocking collectives, body(): sums = lax.all_to_all(sums, ('outer', 'mer'), 0, 0)  16.2 us
    all_to_all x1, blocking collectives, body(): received = lax.all_to_all(message, 'mer', 0, 0)  9.49 us
    ppermute x1, starting transfers between devices, body(): from_other = lax.ppermute(to_other, mode, other)  5.4 us
    ppermute x1, starting transfers between devices, body(): from_pair = lax.ppermute(to_pair, mode, [(i, i ^ 1) for i in range(groups)])  4.07 us
    pallas_call x1, Pallas kernels, body(): pl.pallas_call(functools.partial(inner_kernel, modes), out_shape=(shape((...  2.73 us
    pallas_call x1, Pallas kernels, body(): pl.pallas_call(functools.partial(layout_kernel, group_of, krylov), out_sh...  2.42 us
    pallas_call x1, Pallas kernels, body(): pl.pallas_call(functools.partial(finish_kernel, float(modes * points * su...  1.91 us
  transfers between devices with their start and end apart: 2, of which 0 were waited for; matrix products, arithmetic and copies ran while one was open for 0% of the time, Pallas kernels for 4%

profile of v1, /device:TPU:1, one launch (start us, length us, event | category | flops | bytes accessed | tf_op | source)
XLA Modules:
  0.0 62.6 jit_solution(3035693069582070928)
XLA Ops:
  0.6 0.0 copy-start.5
  0.6 0.7 %copy-done.5 = s32[512]{0:T(512)S(1)} copy-done((s32[512]{0:T(512)S(1)}, s32[512]{0:T(512)}, u32[]{:S(2)}) %copy-start.5) | copy-done | bytes 2072
  1.3 0.0 copy-start
  1.3 0.0 copy-start.1
  1.3 0.0 copy-start.2
  1.3 0.0 copy-start.3
  1.3 0.0 copy-start.4
  1.3 0.0 copy-start.6
  1.3 0.0 copy-start.7
  1.4 2.4 %layout.1 = (s32[2]{0:T(128)S(1)}, f32[2,2,32,256]{3,2,1,0:T(8,128)S(1)}, f32[2,2,32,256]{3,2,1,0:T(8,128)S(1)}) custom-call(s32[4,128]{1,0:T(4,128)S(1)} %bitcast.2, f32[4,2,8,32,256]{4,3,2,1,0:T(8,128)} %basis_ref.7), custom_call_target="tpu_custom_call" | custom-call | flops 10000000000 | bytes 262144 | tf_op jit(solution)/shard_map/layout/pallas_call | solution.py:471
  3.8 5.4 %collective-permute-start = (f32[2,2,32,256]{3,2,1,0:T(8,128)S(1)}, f32[2,2,32,256]{3,2,1,0:T(8,128)S(1)}, u32[]{:S(2)}, u32[]{:S(2)}) collective-permute-start(f32[2,2,32,256]{3,2,1,0:T(8,128)S(1)} %get-tuple-element.20), channel_id=1, source_target_pairs={{4,8},{12,16},{20,24},{28,32},{36,40},{44,48},{52,56},{60,64},{68,... | collective-permute-start | bytes 393224 | tf_op jit(solution)/shard_map/ppermute | solution.py:487
  9.2 4.1 %collective-permute-start.1 = (f32[2,2,32,256]{3,2,1,0:T(8,128)S(1)}, f32[2,2,32,256]{3,2,1,0:T(8,128)S(1)}, u32[]{:S(2)}, u32[]{:S(2)}) collective-permute-start(f32[2,2,32,256]{3,2,1,0:T(8,128)S(1)} %get-tuple-element.21), channel_id=1, source_target_pairs={{0,4},{4,0},{8,12},{12,8},{16,20},{20,16},{24,28},{28,24},{32,36},... | collective-permute-start | bytes 393224 | tf_op jit(solution)/shard_map/ppermute | solution.py:488
  13.3 0.0 copy-done
  13.3 0.0 copy-done.1
  13.3 0.0 copy-done.2
  13.3 0.0 copy-done.3
  13.3 0.0 copy-done.4
  13.3 0.0 copy-done.6
  13.3 0.0 copy-done.7
  13.3 2.7 %inner.1 = (f32[2,8,32,256]{3,2,1,0:T(8,128)S(1)}, f32[2,16,256]{2,1,0:T(8,128)S(1)}, bf16[2,256,256]{2,1,0:T(8,128)(2,1)S(1)}, bf16[2,256,256]{2,1,0:T(8,128)(2...) custom-call(s32[2]{0:T(128)S(1)} %get-tuple-element.19.info_ref, s32[128]{0:T(128)S(1)} %copy-done.6, ...), custom_call_target="tpu_custom_call" | custom-call | flops 1000000000 | bytes 8388608 | tf_op jit(solution)/shard_map/inner/pallas_call | solution.py:491
  16.1 0.0 collective-permute-done.other_ref
  16.1 0.0 collective-permute-done.1.pair_ref
  16.1 1.2 %halo.1 = (f32[2,8,32,256]{3,2,1,0:T(8,128)S(1)}, f32[4,72,256]{2,1,0:T(8,128)S(1)}) custom-call(s32[2]{0:T(128)S(1)} %get-tuple-element.19.info_ref, f32[2,2,32,256]{3,2,1,0:T(8,128)S(1)} %collective-permute-done.other_ref, f32[2,2,32,256]{3,2,1,0:T(8,128)S(1)} %collective-permute-done.1.pair_ref, f32[4,32,256]{2,1,0:T(8,128)S(1)} %copy-done.2, ...), custom_call_target="tpu_custom_call" | custom-call | tf_op jit(solution)/shard_map/halo/pallas_call | solution.py:510
  17.3 9.5 %all_to_all.15.received_ref = f32[4,72,256]{2,1,0:T(8,128)S(1)} all-to-all(f32[4,72,256]{2,1,0:T(8,128)S(1)} %get-tuple-element.26), channel_id=1, replica_groups=mesh['outer'=8,'inner'=16,'mer'=4] {'mer'}, dimensions={0} | all-to-all | bytes 589824 | tf_op jit(solution)/shard_map/all_to_all | solution.py:521
  26.8 1.2 %project.1 = (f32[2,8,32,256]{3,2,1,0:T(8,128)S(1)}, f32[16,1,128]{2,1,0:T(1,128)S(1)}) custom-call(s32[2]{0:T(128)S(1)} %get-tuple-element.19.info_ref, f32[4,72,256]{2,1,0:T(8,128)S(1)} %all_to_all.15.received_ref, f32[1,256]{1,0:T(1,128)S(1)} %get-tuple-element.27.mask_ref, f32[2,32,32]{2,1,0:T(8,128)S(1)} %copy-done.1, ...), custom_call_target="tpu_custom_call" | custom-call | tf_op jit(solution)/shard_map/project/pallas_call | solution.py:524
  28.0 16.5 %all_to_all.16 = f32[16,1,128]{2,1,0:T(1,128)S(1)} all-to-all(f32[16,1,128]{2,1,0:T(1,128)S(1)} %get-tuple-element.30), channel_id=1, replica_groups=mesh['outer'=8,'inner'=16,'mer'=4] {'inner'}, dimensions={0} | all-to-all | bytes 16384 | tf_op jit(solution)/shard_map/all_to_all | solution.py:534
  44.5 16.2 %all_to_all.17.sums_ref = f32[32,1,128]{2,1,0:T(1,128)S(1)} all-to-all(f32[32,1,128]{2,1,0:T(1,128)S(1)} %broadcast_in_dim.2), channel_id=1, replica_groups=mesh['outer'=8,'inner'=16,'mer'=4] {'outer','mer'}, dimensions={0} | all-to-all | bytes 32768 | tf_op jit(solution)/shard_map/all_to_all | solution.py:536
  60.7 1.9 %finish.1 = (f32[2,8,32,256]{3,2,1,0:T(8,128)}, f32[2,4]{1,0:T(2,128)}, f32[1,1]{1,0:T(1,128)}) custom-call(s32[2]{0:T(128)S(1)} %get-tuple-element.19.info_ref, f32[32,1,128]{2,1,0:T(1,128)S(1)} %all_to_all.17.sums_ref, f32[4,2,8,32,256]{4,3,2,1,0:T(8,128)S(1)} %copy-done, f32[2,8,32,256]{3,2,1,0:T(8,128)S(1)} %get-tuple-element.31.w_ref), custom_call_target="tpu_custom_call" | custom-call | tf_op jit(solution)/shard_map/finish/pallas_call | solution.py:538
  (2 shorter events, 0.0 us)
Async XLA Ops:
  0.6 0.7 %copy-start.5 = (s32[512]{0:T(512)S(1)}, s32[512]{0:T(512)}, u32[]{:S(2)}) copy-start(s32[512]{0:T(512)} %param.8) | copy-start | bytes 6148
  1.3 11.9 %copy-start = (f32[4,2,8,32,256]{4,3,2,1,0:T(8,128)S(1)}, f32[4,2,8,32,256]{4,3,2,1,0:T(8,128)}, u32[]{:S(2)}) copy-start(f32[4,2,8,32,256]{4,3,2,1,0:T(8,128)} %basis_ref.7) | copy-start | bytes 6291460
  1.3 12.0 %copy-start.1 = (f32[2,32,32]{2,1,0:T(8,128)S(1)}, f32[2,32,32]{2,1,0:T(8,128)}, u32[]{:S(2)}) copy-start(f32[2,32,32]{2,1,0:T(8,128)} %axial_ref.5) | copy-start | bytes 24580
  1.3 12.0 %copy-start.2 = (f32[4,32,256]{2,1,0:T(8,128)S(1)}, f32[4,32,256]{2,1,0:T(8,128)}, u32[]{:S(2)}) copy-start(f32[4,32,256]{2,1,0:T(8,128)} %flow_ref.3) | copy-start | bytes 393220
  1.3 12.0 %copy-start.3 = (f32[2,256,256]{2,1,0:T(8,128)S(1)}, f32[2,256,256]{2,1,0:T(8,128)}, u32[]{:S(2)}) copy-start(f32[2,256,256]{2,1,0:T(8,128)} %radial_ref.1) | copy-start | bytes 1572868
  1.3 12.0 %copy-start.4 = (f32[32,256]{1,0:T(8,128)S(1)}, f32[32,256]{1,0:T(8,128)}, u32[]{:S(2)}) copy-start(f32[32,256]{1,0:T(8,128)} %swirl_ref.1) | copy-start | bytes 98308
  1.3 12.0 %copy-start.6 = (s32[128]{0:T(128)S(1)}, s32[128]{0:T(128)}, u32[]{:S(2)}) copy-start(s32[128]{0:T(128)} %iface_ref.1) | copy-start | bytes 1540
  1.3 12.0 %copy-start.7 = (f32[2]{0:T(128)S(1)}, f32[2]{0:T(128)}, u32[]{:S(2)}) copy-start(f32[2]{0:T(128)} %shift_ref.1) | copy-start | bytes 28
  3.8 12.3 %collective-permute-start = (f32[2,2,32,256]{3,2,1,0:T(8,128)S(1)}, f32[2,2,32,256]{3,2,1,0:T(8,128)S(1)}, u32[]{:S(2)}, u32[]{:S(2)}) collective-permute-start(f32[2,2,32,256]{3,2,1,0:T(8,128)S(1)} %get-tuple-element.20), channel_id=1, source_target_pairs={{4,8},{12,16},{20,24},{28,32},{36,40},{44,48},{52,56},{60,64},{68,... | collective-permute-start | bytes 393224 | tf_op jit(solution)/shard_map/ppermute | solution.py:487
  9.2 6.9 %collective-permute-start.1 = (f32[2,2,32,256]{3,2,1,0:T(8,128)S(1)}, f32[2,2,32,256]{3,2,1,0:T(8,128)S(1)}, u32[]{:S(2)}, u32[]{:S(2)}) collective-permute-start(f32[2,2,32,256]{3,2,1,0:T(8,128)S(1)} %get-tuple-element.21), channel_id=1, source_target_pairs={{0,4},{4,0},{8,12},{12,8},{16,20},{20,16},{24,28},{28,24},{32,36},... | collective-permute-start | bytes 393224 | tf_op jit(solution)/shard_map/ppermute | solution.py:488

commit v2 on v1

--- a/solution.py
+++ b/solution.py
@@ -30,10 +30,10 @@
 
 
 def dot3(a, b, dims):
-    def one(x, y):
-        return lax.dot_general(x, y, dims, preferred_element_type=F32)
-
-    return one(a[0], b[0]) + (one(a[0], b[1]) + one(a[1], b[0]))
+    along = dims[0][1][0]
+    left = jnp.concatenate([a[0], a[0], a[1]], axis=1)
+    right = jnp.concatenate([b[0], b[1], b[0]], axis=along)
+    return lax.dot_general(left, right, dims, preferred_element_type=F32)
 
 
 def block_diagonal(block, copies):
@@ -163,12 +163,12 @@
         gram = gram + jnp.where(lane == 2 * krylov + 1 + i, jnp.sum(s, keepdims=True), 0.0)
     gram_ref[...] = gram
 
-    column = lax.broadcasted_iota(jnp.int32, (1, width), 1)
-
-    def mark(i, mask):
-        return jnp.where(column == iface_ref[i], 1.0, mask)
-
-    mask_ref[...] = lax.fori_loop(0, iface_ref.shape[0], mark, jnp.zeros((1, width), F32), unroll=8)
+    chosen = iface_ref[...].astype(F32)
+    chosen = jnp.broadcast_to(chosen, (chosen.shape[1], chosen.shape[1])).T
+    for c in range(0, width, chosen.shape[1]):
+        column = lax.broadcasted_iota(jnp.int32, chosen.shape, 1) + c
+        hits = jnp.where(chosen == column.astype(F32), 1.0, 0.0)
+        mask_ref[:, c : c + chosen.shape[1]] = jnp.sum(hits, axis=0, keepdims=True)
 
     first_block = block_diagonal(axial_ref[0], slots)
     second_block = block_diagonal(axial_ref[1], slots)
@@ -498,13 +498,13 @@
             shape((1, 128), F32),
             shape((1, width), F32),
         ),
-        in_specs=[SMEM, SMEM, SMEM, VMEM, VMEM, VMEM, VMEM, VMEM],
+        in_specs=[SMEM, VMEM, SMEM, VMEM, VMEM, VMEM, VMEM, VMEM],
         out_specs=(VMEM,) * 6,
         scratch_shapes=[pltpu.VMEM((2, rows, width), BF16)] * 2,
         compiler_params=params(),
         cost_estimate=pl.CostEstimate(flops=10**9, bytes_accessed=8 * 2**20, transcendentals=0),
         name="inner",
-    )(info, iface_index, shift, basis, radial, axial, flow_coupling, swirl)
+    )(info, iface_index.reshape(1, -1), shift, basis, radial, axial, flow_coupling, swirl)
 
     wide = 2 * slots
     local, message = pl.pallas_call(

time: 62.9 us -> 62.6 us (level)
  no operation moved by 1% of the time
where the time goes in v2:
time: 62.6 us; the launch traced here: 62.4 us
  blocking collectives  42.1 us (67%)
  starting transfers between devices  9.46 us (15%)
  Pallas kernels  9.23 us (15%)
  between operations  0.78 us (1%)
  local copies, waits for them, and re-layouts  0.72 us (1%)
    all_to_all x1, blocking collectives, body(): sums = lax.all_to_all(sums, 'inner', 0, 0)  16.4 us
    all_to_all x1, blocking collectives, body(): sums = lax.all_to_all(sums, ('outer', 'mer'), 0, 0)  16.2 us
    all_to_all x1, blocking collectives, body(): received = lax.all_to_all(message, 'mer', 0, 0)  9.49 us
    ppermute x1, starting transfers between devices, body(): from_other = lax.ppermute(to_other, mode, other)  5.4 us
    ppermute x1, starting transfers between devices, body(): from_pair = lax.ppermute(to_pair, mode, [(i, i ^ 1) for i in range(groups)])  4.07 us
    pallas_call x1, Pallas kernels, body(): pl.pallas_call(functools.partial(inner_kernel, modes), out_shape=(shape((...  2.48 us
    pallas_call x1, Pallas kernels, body(): pl.pallas_call(functools.partial(layout_kernel, group_of, krylov), out_sh...  2.42 us
    pallas_call x1, Pallas kernels, body(): pl.pallas_call(functools.partial(finish_kernel, float(modes * points * su...  1.91 us
  transfers between devices with their start and end apart: 2, of which 0 were waited for; matrix products, arithmetic and copies ran while one was open for 0% of the time, Pallas kernels for 4%

profile of v2, /device:TPU:1, one launch (start us, length us, event | category | flops | bytes accessed | tf_op | source)
XLA Modules:
  0.0 62.4 jit_solution(13074911261544523986)
XLA Ops:
  0.6 0.0 copy-start.5
  0.6 0.7 %copy-done.5 = s32[512]{0:T(512)S(1)} copy-done((s32[512]{0:T(512)S(1)}, s32[512]{0:T(512)}, u32[]{:S(2)}) %copy-start.5) | copy-done | bytes 2072
  1.3 0.0 copy-start
  1.3 0.0 copy-start.1
  1.3 0.0 copy-start.2
  1.3 0.0 copy-start.3
  1.3 0.0 copy-start.4
  1.3 0.0 copy-start.6
  1.3 0.0 copy-start.7
  1.4 2.4 %layout.1 = (s32[2]{0:T(128)S(1)}, f32[2,2,32,256]{3,2,1,0:T(8,128)S(1)}, f32[2,2,32,256]{3,2,1,0:T(8,128)S(1)}) custom-call(s32[4,128]{1,0:T(4,128)S(1)} %bitcast.3, f32[4,2,8,32,256]{4,3,2,1,0:T(8,128)} %basis_ref.7), custom_call_target="tpu_custom_call" | custom-call | flops 10000000000 | bytes 262144 | tf_op jit(solution)/shard_map/layout/pallas_call | solution.py:471
  3.8 5.4 %collective-permute-start = (f32[2,2,32,256]{3,2,1,0:T(8,128)S(1)}, f32[2,2,32,256]{3,2,1,0:T(8,128)S(1)}, u32[]{:S(2)}, u32[]{:S(2)}) collective-permute-start(f32[2,2,32,256]{3,2,1,0:T(8,128)S(1)} %get-tuple-element.20), channel_id=1, source_target_pairs={{4,8},{12,16},{20,24},{28,32},{36,40},{44,48},{52,56},{60,64},{68,... | collective-permute-start | bytes 393224 | tf_op jit(solution)/shard_map/ppermute | solution.py:487
  9.2 4.1 %collective-permute-start.1 = (f32[2,2,32,256]{3,2,1,0:T(8,128)S(1)}, f32[2,2,32,256]{3,2,1,0:T(8,128)S(1)}, u32[]{:S(2)}, u32[]{:S(2)}) collective-permute-start(f32[2,2,32,256]{3,2,1,0:T(8,128)S(1)} %get-tuple-element.21), channel_id=1, source_target_pairs={{0,4},{4,0},{8,12},{12,8},{16,20},{20,16},{24,28},{28,24},{32,36},... | collective-permute-start | bytes 393224 | tf_op jit(solution)/shard_map/ppermute | solution.py:488
  13.3 0.0 copy-done
  13.3 0.0 copy-done.1
  13.3 0.0 copy-done.2
  13.3 0.0 copy-done.3
  13.3 0.0 copy-done.4
  13.3 0.0 copy-done.6
  13.3 0.0 copy-done.7
  13.3 2.5 %inner.1 = (f32[2,8,32,256]{3,2,1,0:T(8,128)S(1)}, f32[2,16,256]{2,1,0:T(8,128)S(1)}, bf16[2,256,256]{2,1,0:T(8,128)(2,1)S(1)}, bf16[2,256,256]{2,1,0:T(8,128)(2...) custom-call(s32[2]{0:T(128)S(1)} %get-tuple-element.19.info_ref, s32[1,128]{1,0:T(1,128)S(1)} %bitcast.4, ...), custom_call_target="tpu_custom_call" | custom-call | flops 1000000000 | bytes 8388608 | tf_op jit(solution)/shard_map/inner/pallas_call | solution.py:491
  15.8 0.0 collective-permute-done.other_ref
  15.8 0.0 collective-permute-done.1.pair_ref
  15.8 1.2 %halo.1 = (f32[2,8,32,256]{3,2,1,0:T(8,128)S(1)}, f32[4,72,256]{2,1,0:T(8,128)S(1)}) custom-call(s32[2]{0:T(128)S(1)} %get-tuple-element.19.info_ref, f32[2,2,32,256]{3,2,1,0:T(8,128)S(1)} %collective-permute-done.other_ref, f32[2,2,32,256]{3,2,1,0:T(8,128)S(1)} %collective-permute-done.1.pair_ref, f32[4,32,256]{2,1,0:T(8,128)S(1)} %copy-done.2, ...), custom_call_target="tpu_custom_call" | custom-call | tf_op jit(solution)/shard_map/halo/pallas_call | solution.py:510
  17.0 9.5 %all_to_all.15.received_ref = f32[4,72,256]{2,1,0:T(8,128)S(1)} all-to-all(f32[4,72,256]{2,1,0:T(8,128)S(1)} %get-tuple-element.26), channel_id=1, replica_groups=mesh['outer'=8,'inner'=16,'mer'=4] {'mer'}, dimensions={0} | all-to-all | bytes 589824 | tf_op jit(solution)/shard_map/all_to_all | solution.py:521
  26.5 1.2 %project.1 = (f32[2,8,32,256]{3,2,1,0:T(8,128)S(1)}, f32[16,1,128]{2,1,0:T(1,128)S(1)}) custom-call(s32[2]{0:T(128)S(1)} %get-tuple-element.19.info_ref, f32[4,72,256]{2,1,0:T(8,128)S(1)} %all_to_all.15.received_ref, f32[1,256]{1,0:T(1,128)S(1)} %get-tuple-element.27.mask_ref, f32[2,32,32]{2,1,0:T(8,128)S(1)} %copy-done.1, ...), custom_call_target="tpu_custom_call" | custom-call | tf_op jit(solution)/shard_map/project/pallas_call | solution.py:524
  27.8 16.4 %all_to_all.16 = f32[16,1,128]{2,1,0:T(1,128)S(1)} all-to-all(f32[16,1,128]{2,1,0:T(1,128)S(1)} %get-tuple-element.30), channel_id=1, replica_groups=mesh['outer'=8,'inner'=16,'mer'=4] {'inner'}, dimensions={0} | all-to-all | bytes 16384 | tf_op jit(solution)/shard_map/all_to_all | solution.py:534
  44.2 16.2 %all_to_all.17.sums_ref = f32[32,1,128]{2,1,0:T(1,128)S(1)} all-to-all(f32[32,1,128]{2,1,0:T(1,128)S(1)} %broadcast_in_dim.2), channel_id=1, replica_groups=mesh['outer'=8,'inner'=16,'mer'=4] {'outer','mer'}, dimensions={0} | all-to-all | bytes 32768 | tf_op jit(solution)/shard_map/all_to_all | solution.py:536
  60.4 1.9 %finish.1 = (f32[2,8,32,256]{3,2,1,0:T(8,128)}, f32[2,4]{1,0:T(2,128)}, f32[1,1]{1,0:T(1,128)}) custom-call(s32[2]{0:T(128)S(1)} %get-tuple-element.19.info_ref, f32[32,1,128]{2,1,0:T(1,128)S(1)} %all_to_all.17.sums_ref, f32[4,2,8,32,256]{4,3,2,1,0:T(8,128)S(1)} %copy-done, f32[2,8,32,256]{3,2,1,0:T(8,128)S(1)} %get-tuple-element.31.w_ref), custom_call_target="tpu_custom_call" | custom-call | tf_op jit(solution)/shard_map/finish/pallas_call | solution.py:538
  (2 shorter events, 0.0 us)
Async XLA Ops:
  0.6 0.7 %copy-start.5 = (s32[512]{0:T(512)S(1)}, s32[512]{0:T(512)}, u32[]{:S(2)}) copy-start(s32[512]{0:T(512)} %param.8) | copy-start | bytes 6148
  1.3 11.9 %copy-start = (f32[4,2,8,32,256]{4,3,2,1,0:T(8,128)S(1)}, f32[4,2,8,32,256]{4,3,2,1,0:T(8,128)}, u32[]{:S(2)}) copy-start(f32[4,2,8,32,256]{4,3,2,1,0:T(8,128)} %basis_ref.7) | copy-start | bytes 6291460
  1.3 12.0 %copy-start.1 = (f32[2,32,32]{2,1,0:T(8,128)S(1)}, f32[2,32,32]{2,1,0:T(8,128)}, u32[]{:S(2)}) copy-start(f32[2,32,32]{2,1,0:T(8,128)} %axial_ref.5) | copy-start | bytes 24580
  1.3 12.0 %copy-start.2 = (f32[4,32,256]{2,1,0:T(8,128)S(1)}, f32[4,32,256]{2,1,0:T(8,128)}, u32[]{:S(2)}) copy-start(f32[4,32,256]{2,1,0:T(8,128)} %flow_ref.3) | copy-start | bytes 393220
  1.3 12.0 %copy-start.3 = (f32[2,256,256]{2,1,0:T(8,128)S(1)}, f32[2,256,256]{2,1,0:T(8,128)}, u32[]{:S(2)}) copy-start(f32[2,256,256]{2,1,0:T(8,128)} %radial_ref.1) | copy-start | bytes 1572868
  1.3 12.0 %copy-start.4 = (f32[32,256]{1,0:T(8,128)S(1)}, f32[32,256]{1,0:T(8,128)}, u32[]{:S(2)}) copy-start(f32[32,256]{1,0:T(8,128)} %swirl_ref.1) | copy-start | bytes 98308
  1.3 12.0 %copy-start.6 = (s32[128]{0:T(128)S(1)}, s32[128]{0:T(128)}, u32[]{:S(2)}) copy-start(s32[128]{0:T(128)} %param.9) | copy-start | bytes 1540
  1.3 12.0 %copy-start.7 = (f32[2]{0:T(128)S(1)}, f32[2]{0:T(128)}, u32[]{:S(2)}) copy-start(f32[2]{0:T(128)} %shift_ref.1) | copy-start | bytes 28
  3.8 12.0 %collective-permute-start = (f32[2,2,32,256]{3,2,1,0:T(8,128)S(1)}, f32[2,2,32,256]{3,2,1,0:T(8,128)S(1)}, u32[]{:S(2)}, u32[]{:S(2)}) collective-permute-start(f32[2,2,32,256]{3,2,1,0:T(8,128)S(1)} %get-tuple-element.20), channel_id=1, source_target_pairs={{4,8},{12,16},{20,24},{28,32},{36,40},{44,48},{52,56},{60,64},{68,... | collective-permute-start | bytes 393224 | tf_op jit(solution)/shard_map/ppermute | solution.py:487
  9.2 6.6 %collective-permute-start.1 = (f32[2,2,32,256]{3,2,1,0:T(8,128)S(1)}, f32[2,2,32,256]{3,2,1,0:T(8,128)S(1)}, u32[]{:S(2)}, u32[]{:S(2)}) collective-permute-start(f32[2,2,32,256]{3,2,1,0:T(8,128)S(1)} %get-tuple-element.21), channel_id=1, source_target_pairs={{0,4},{4,0},{8,12},{12,8},{16,20},{20,16},{24,28},{28,24},{32,36},... | collective-permute-start | bytes 393224 | tf_op jit(solution)/shard_map/ppermute | solution.py:488

commit v3 on v2

--- a/solution.py
+++ b/solution.py
@@ -54,24 +54,11 @@
     return parts
 
 
-def layout_kernel(group_of, krylov, cost_ref, basis_ref, info_ref, other_ref, pair_ref, sems):
+def layout_kernel(group_of, krylov, cost_ref, basis_ref, info_ref, other_ref, pair_ref, vector_ref, sem):
     group = group_of()
     even = lax.rem(group, 2) == 0
-
-    def copy(at, ref, which, part):
-        return pltpu.make_async_copy(
-            basis_ref.at[krylov - 1, part, pl.ds(at, 2)], ref.at[part], sems.at[which, part]
-        )
-
-    @pl.when(even)
-    def _():
-        for part in range(2):
-            copy(0, other_ref, 0, part).start()
-
-    @pl.when(jnp.logical_not(even))
-    def _():
-        for part in range(2):
-            copy(0, pair_ref, 0, part).start()
+    fetch = pltpu.make_async_copy(basis_ref.at[krylov - 1], vector_ref, sem)
+    fetch.start()
 
     cost = cost_ref[...]
     rows, lanes = cost.shape
@@ -92,23 +79,16 @@
     start = lax.rem(both, base)
     count = lax.div(both, base) - start
 
-    top = jnp.maximum(count - 2, 0)
-
-    @pl.when(even)
-    def _():
-        for part in range(2):
-            copy(top, pair_ref, 1, part).start()
-
-    @pl.when(jnp.logical_not(even))
-    def _():
-        for part in range(2):
-            copy(top, other_ref, 1, part).start()
-
     info_ref[0] = count
     info_ref[1] = start
-    for which in range(2):
-        for part in range(2):
-            copy(0, pair_ref, which, part).wait()
+    top = jnp.maximum(count - 2, 0)
+    to_pair = jnp.where(even, top, 0)
+    to_other = jnp.where(even, 0, top)
+    fetch.wait()
+    for part in range(2):
+        for i in range(2):
+            other_ref[part, i] = vector_ref[part, to_other + i]
+            pair_ref[part, i] = vector_ref[part, to_pair + i]
 
 
 def inner_kernel(
@@ -390,7 +370,8 @@
     )
     lane = lax.broadcasted_iota(jnp.int32, (1, 128), 1)
     out = gram_ref[...]
-    for i, s in enumerate(sums):
+    order = [i // 2 + krylov * (i % 2) for i in range(2 * krylov)] + [2 * krylov]
+    for i, s in zip(order, sums):
         out = out + jnp.where(lane == i, jnp.sum(s, keepdims=True), 0.0)
     for to in range(sums_ref.shape[0]):
         sums_ref[to] = out
@@ -404,8 +385,8 @@
     def at(i):
         return total[:, i : i + 1]
 
-    re = [at(2 * k) for k in range(krylov)]
-    im = [at(2 * k + 1) for k in range(krylov)]
+    re = [at(k) for k in range(krylov)]
+    im = [at(krylov + k) for k in range(krylov)]
     squares = at(2 * krylov)
     place = 2 * krylov + 1
     for i in range(krylov):
@@ -421,9 +402,8 @@
                 place += 2
     norm = jnp.sqrt(squares + EPSILON)
     norm_ref[...] = norm
-    coeffs_ref[...] = jnp.concatenate(
-        [jnp.concatenate(re, axis=1), jnp.concatenate(im, axis=1)], axis=0
-    )
+    coeffs_ref[0:1] = total[:, 0:krylov]
+    coeffs_ref[1:2] = total[:, krylov : 2 * krylov]
     scale = jnp.broadcast_to(1.0 / norm, (8, 128))
     re = [jnp.broadcast_to(x, (8, 128)) for x in re]
     im = [jnp.broadcast_to(x, (8, 128)) for x in im]
@@ -477,7 +457,7 @@
         ),
         in_specs=[VMEM, ANY],
         out_specs=(SMEM, VMEM, VMEM),
-        scratch_shapes=[pltpu.SemaphoreType.DMA((2, 2))],
+        scratch_shapes=[pltpu.VMEM((2, slots, points, width), F32), pltpu.SemaphoreType.DMA],
         compiler_params=params(52),
         cost_estimate=pl.CostEstimate(flops=10**10, bytes_accessed=2**18, transcendentals=0),
         name="layout",

time: 62.6 us -> 62.5 us (level)
    all_to_all x1, blocking collectives: 16.4 us -> 17.4 us  [body(): sums = lax.all_to_all(sums, 'inner', 0, 0)]
where the time goes in v3:
time: 62.5 us; the launch traced here: 62.2 us
  blocking collectives  42.6 us (68%)
  starting transfers between devices  9.46 us (15%)
  Pallas kernels  8.64 us (14%)
  between operations  0.78 us (1%)
  local copies, waits for them, and re-layouts  0.72 us (1%)
    all_to_all x1, blocking collectives, body(): sums = lax.all_to_all(sums, 'inner', 0, 0)  17.4 us
    all_to_all x1, blocking collectives, body(): sums = lax.all_to_all(sums, ('outer', 'mer'), 0, 0)  16.2 us
    all_to_all x1, blocking collectives, body(): received = lax.all_to_all(message, 'mer', 0, 0)  9 us
    ppermute x1, starting transfers between devices, body(): from_other = lax.ppermute(to_other, mode, other)  5.39 us
    ppermute x1, starting transfers between devices, body(): from_pair = lax.ppermute(to_pair, mode, [(i, i ^ 1) for i in range(groups)])  4.07 us
    pallas_call x1, Pallas kernels, body(): pl.pallas_call(functools.partial(inner_kernel, modes), out_shape=(shape((...  2.34 us
    pallas_call x1, Pallas kernels, body(): pl.pallas_call(functools.partial(layout_kernel, group_of, krylov), out_sh...  2.29 us
    pallas_call x1, Pallas kernels, body(): pl.pallas_call(functools.partial(finish_kernel, float(modes * points * su...  1.84 us
  transfers between devices with their start and end apart: 2, of which 0 were waited for; matrix products, arithmetic and copies ran while one was open for 0% of the time, Pallas kernels for 4%

profile of v3, /device:TPU:1, one launch (start us, length us, event | category | flops | bytes accessed | tf_op | source)
XLA Modules:
  0.0 62.2 jit_solution(17748407518357228876)
XLA Ops:
  0.6 0.0 copy-start.5
  0.6 0.7 %copy-done.5 = s32[512]{0:T(512)S(1)} copy-done((s32[512]{0:T(512)S(1)}, s32[512]{0:T(512)}, u32[]{:S(2)}) %copy-start.5) | copy-done | bytes 2072
  1.3 0.0 copy-start
  1.3 0.0 copy-start.1
  1.3 0.0 copy-start.2
  1.3 0.0 copy-start.3
  1.3 0.0 copy-start.4
  1.3 0.0 copy-start.6
  1.3 0.0 copy-start.7
  1.4 2.3 %layout.1 = (s32[2]{0:T(128)S(1)}, f32[2,2,32,256]{3,2,1,0:T(8,128)S(1)}, f32[2,2,32,256]{3,2,1,0:T(8,128)S(1)}) custom-call(s32[4,128]{1,0:T(4,128)S(1)} %bitcast.3, f32[4,2,8,32,256]{4,3,2,1,0:T(8,128)} %basis_ref.7), custom_call_target="tpu_custom_call" | custom-call | flops 10000000000 | bytes 262144 | tf_op jit(solution)/shard_map/layout/pallas_call | solution.py:451
  3.7 5.4 %collective-permute-start = (f32[2,2,32,256]{3,2,1,0:T(8,128)S(1)}, f32[2,2,32,256]{3,2,1,0:T(8,128)S(1)}, u32[]{:S(2)}, u32[]{:S(2)}) collective-permute-start(f32[2,2,32,256]{3,2,1,0:T(8,128)S(1)} %get-tuple-element.20), channel_id=1, source_target_pairs={{4,8},{12,16},{20,24},{28,32},{36,40},{44,48},{52,56},{60,64},{68,... | collective-permute-start | bytes 393224 | tf_op jit(solution)/shard_map/ppermute | solution.py:467
  9.0 4.1 %collective-permute-start.1 = (f32[2,2,32,256]{3,2,1,0:T(8,128)S(1)}, f32[2,2,32,256]{3,2,1,0:T(8,128)S(1)}, u32[]{:S(2)}, u32[]{:S(2)}) collective-permute-start(f32[2,2,32,256]{3,2,1,0:T(8,128)S(1)} %get-tuple-element.21), channel_id=1, source_target_pairs={{0,4},{4,0},{8,12},{12,8},{16,20},{20,16},{24,28},{28,24},{32,36},... | collective-permute-start | bytes 393224 | tf_op jit(solution)/shard_map/ppermute | solution.py:468
  13.1 0.0 copy-done
  13.1 0.0 copy-done.1
  13.1 0.0 copy-done.2
  13.2 0.0 copy-done.3
  13.2 0.0 copy-done.4
  13.2 0.0 copy-done.6
  13.2 0.0 copy-done.7
  13.2 2.3 %inner.1 = (f32[2,8,32,256]{3,2,1,0:T(8,128)S(1)}, f32[2,16,256]{2,1,0:T(8,128)S(1)}, bf16[2,256,256]{2,1,0:T(8,128)(2,1)S(1)}, bf16[2,256,256]{2,1,0:T(8,128)(2...) custom-call(s32[2]{0:T(128)S(1)} %get-tuple-element.19.info_ref, s32[1,128]{1,0:T(1,128)S(1)} %bitcast.4, ...), custom_call_target="tpu_custom_call" | custom-call | flops 1000000000 | bytes 8388608 | tf_op jit(solution)/shard_map/inner/pallas_call | solution.py:471
  15.5 0.0 collective-permute-done.other_ref
  15.5 0.0 collective-permute-done.1.pair_ref
  15.5 1.2 %halo.1 = (f32[2,8,32,256]{3,2,1,0:T(8,128)S(1)}, f32[4,72,256]{2,1,0:T(8,128)S(1)}) custom-call(s32[2]{0:T(128)S(1)} %get-tuple-element.19.info_ref, f32[2,2,32,256]{3,2,1,0:T(8,128)S(1)} %collective-permute-done.other_ref, f32[2,2,32,256]{3,2,1,0:T(8,128)S(1)} %collective-permute-done.1.pair_ref, f32[4,32,256]{2,1,0:T(8,128)S(1)} %copy-done.2, ...), custom_call_target="tpu_custom_call" | custom-call | tf_op jit(solution)/shard_map/halo/pallas_call | solution.py:490
  16.8 9.0 %all_to_all.15.received_ref = f32[4,72,256]{2,1,0:T(8,128)S(1)} all-to-all(f32[4,72,256]{2,1,0:T(8,128)S(1)} %get-tuple-element.26), channel_id=1, replica_groups=mesh['outer'=8,'inner'=16,'mer'=4] {'mer'}, dimensions={0} | all-to-all | bytes 589824 | tf_op jit(solution)/shard_map/all_to_all | solution.py:501
  25.8 1.0 %project.1 = (f32[2,8,32,256]{3,2,1,0:T(8,128)S(1)}, f32[16,1,128]{2,1,0:T(1,128)S(1)}) custom-call(s32[2]{0:T(128)S(1)} %get-tuple-element.19.info_ref, f32[4,72,256]{2,1,0:T(8,128)S(1)} %all_to_all.15.received_ref, f32[1,256]{1,0:T(1,128)S(1)} %get-tuple-element.27.mask_ref, f32[2,32,32]{2,1,0:T(8,128)S(1)} %copy-done.1, ...), custom_call_target="tpu_custom_call" | custom-call | tf_op jit(solution)/shard_map/project/pallas_call | solution.py:504
  26.7 17.4 %all_to_all.16 = f32[16,1,128]{2,1,0:T(1,128)S(1)} all-to-all(f32[16,1,128]{2,1,0:T(1,128)S(1)} %get-tuple-element.30), channel_id=1, replica_groups=mesh['outer'=8,'inner'=16,'mer'=4] {'inner'}, dimensions={0} | all-to-all | bytes 16384 | tf_op jit(solution)/shard_map/all_to_all | solution.py:514
  44.1 16.2 %all_to_all.17.sums_ref = f32[32,1,128]{2,1,0:T(1,128)S(1)} all-to-all(f32[32,1,128]{2,1,0:T(1,128)S(1)} %broadcast_in_dim.2), channel_id=1, replica_groups=mesh['outer'=8,'inner'=16,'mer'=4] {'outer','mer'}, dimensions={0} | all-to-all | bytes 32768 | tf_op jit(solution)/shard_map/all_to_all | solution.py:516
  60.3 1.8 %finish.1 = (f32[2,8,32,256]{3,2,1,0:T(8,128)}, f32[2,4]{1,0:T(2,128)}, f32[1,1]{1,0:T(1,128)}) custom-call(s32[2]{0:T(128)S(1)} %get-tuple-element.19.info_ref, f32[32,1,128]{2,1,0:T(1,128)S(1)} %all_to_all.17.sums_ref, f32[4,2,8,32,256]{4,3,2,1,0:T(8,128)S(1)} %copy-done, f32[2,8,32,256]{3,2,1,0:T(8,128)S(1)} %get-tuple-element.31.w_ref), custom_call_target="tpu_custom_call" | custom-call | tf_op jit(solution)/shard_map/finish/pallas_call | solution.py:518
  (2 shorter events, 0.0 us)
Async XLA Ops:
  0.6 0.7 %copy-start.5 = (s32[512]{0:T(512)S(1)}, s32[512]{0:T(512)}, u32[]{:S(2)}) copy-start(s32[512]{0:T(512)} %param.8) | copy-start | bytes 6148
  1.3 11.8 %copy-start = (f32[4,2,8,32,256]{4,3,2,1,0:T(8,128)S(1)}, f32[4,2,8,32,256]{4,3,2,1,0:T(8,128)}, u32[]{:S(2)}) copy-start(f32[4,2,8,32,256]{4,3,2,1,0:T(8,128)} %basis_ref.7) | copy-start | bytes 6291460
  1.3 11.8 %copy-start.1 = (f32[2,32,32]{2,1,0:T(8,128)S(1)}, f32[2,32,32]{2,1,0:T(8,128)}, u32[]{:S(2)}) copy-start(f32[2,32,32]{2,1,0:T(8,128)} %axial_ref.5) | copy-start | bytes 24580
  1.3 11.8 %copy-start.2 = (f32[4,32,256]{2,1,0:T(8,128)S(1)}, f32[4,32,256]{2,1,0:T(8,128)}, u32[]{:S(2)}) copy-start(f32[4,32,256]{2,1,0:T(8,128)} %flow_ref.3) | copy-start | bytes 393220
  1.3 11.8 %copy-start.3 = (f32[2,256,256]{2,1,0:T(8,128)S(1)}, f32[2,256,256]{2,1,0:T(8,128)}, u32[]{:S(2)}) copy-start(f32[2,256,256]{2,1,0:T(8,128)} %radial_ref.1) | copy-start | bytes 1572868
  1.3 11.8 %copy-start.4 = (f32[32,256]{1,0:T(8,128)S(1)}, f32[32,256]{1,0:T(8,128)}, u32[]{:S(2)}) copy-start(f32[32,256]{1,0:T(8,128)} %swirl_ref.1) | copy-start | bytes 98308
  1.3 11.8 %copy-start.6 = (s32[128]{0:T(128)S(1)}, s32[128]{0:T(128)}, u32[]{:S(2)}) copy-start(s32[128]{0:T(128)} %param.9) | copy-start | bytes 1540
  1.3 11.8 %copy-start.7 = (f32[2]{0:T(128)S(1)}, f32[2]{0:T(128)}, u32[]{:S(2)}) copy-start(f32[2]{0:T(128)} %shift_ref.1) | copy-start | bytes 28
  3.7 11.9 %collective-permute-start = (f32[2,2,32,256]{3,2,1,0:T(8,128)S(1)}, f32[2,2,32,256]{3,2,1,0:T(8,128)S(1)}, u32[]{:S(2)}, u32[]{:S(2)}) collective-permute-start(f32[2,2,32,256]{3,2,1,0:T(8,128)S(1)} %get-tuple-element.20), channel_id=1, source_target_pairs={{4,8},{12,16},{20,24},{28,32},{36,40},{44,48},{52,56},{60,64},{68,... | collective-permute-start | bytes 393224 | tf_op jit(solution)/shard_map/ppermute | solution.py:467
  9.0 6.5 %collective-permute-start.1 = (f32[2,2,32,256]{3,2,1,0:T(8,128)S(1)}, f32[2,2,32,256]{3,2,1,0:T(8,128)S(1)}, u32[]{:S(2)}, u32[]{:S(2)}) collective-permute-start(f32[2,2,32,256]{3,2,1,0:T(8,128)S(1)} %get-tuple-element.21), channel_id=1, source_target_pairs={{0,4},{4,0},{8,12},{12,8},{16,20},{20,16},{24,28},{28,24},{32,36},... | collective-permute-start | bytes 393224 | tf_op jit(solution)/shard_map/ppermute | solution.py:468

commit v4 on v2

--- a/solution.py
+++ b/solution.py
@@ -243,6 +243,7 @@
     radial1_ref,
     ends_ref,
     axial_ref,
+    mask_ref,
     before_ref,
     local_ref,
     message_ref,
@@ -284,20 +285,21 @@
             for i in (points - 1, 0)
             for j in (0, points - 1)
         ]
-        + [jnp.zeros((4, width), F32)],
+        + [jnp.zeros((wide - 4, width), F32)],
         axis=0,
     )
+    top = jnp.where(mask_ref[...] > 0.0, traces[0], corners)
     for to in range(message_ref.shape[0]):
-        message_ref[to, 0:wide] = traces[0]
+        message_ref[to, 0:wide] = top
         message_ref[to, wide : 2 * wide] = traces[1]
         message_ref[to, 2 * wide : 3 * wide] = ends_ref[0]
         message_ref[to, 3 * wide : 4 * wide] = ends_ref[1]
-        message_ref[to, 4 * wide :] = corners
 
 
 def project_kernel(
     sub_of,
     inverse,
+    free,
     info_ref,
     received_ref,
     mask_ref,
@@ -314,6 +316,7 @@
     wide = 2 * slots
     count = info_ref[0]
     sub = sub_of()
+    chosen = mask_ref[...] > 0.0
     after = [received_ref[s, 2 * wide : 3 * wide] for s in range(subs)]
     before = [received_ref[s, 3 * wide : 4 * wide] for s in range(subs)]
     tops = []
@@ -321,7 +324,7 @@
     for s in range(subs):
         top = received_ref[s, 0:wide]
         bottom = received_ref[s, wide : 2 * wide]
-        corner = received_ref[s, 4 * wide :]
+        corner = jnp.sum(jnp.where(chosen, 0.0, top[0:8]), axis=1, keepdims=True) / free
         if s > 0:
             top = top + PENALTY * corner[0:1] * after[s - 1]
             bottom = bottom + PENALTY * corner[2:3] * after[s - 1]
@@ -330,7 +333,7 @@
             bottom = bottom + PENALTY * corner[3:4] * before[s + 1]
         tops.append(top)
         bottoms.append(bottom)
-    jumps = [(tops[j - 1] - bottoms[j]) * mask_ref[...] for j in range(1, subs)]
+    jumps = [jnp.where(chosen, tops[j - 1] - bottoms[j], 0.0) for j in range(1, subs)]
 
     def solved(at):
         g = jnp.zeros((wide, width), F32)
@@ -511,18 +514,20 @@
         functools.partial(halo_kernel, group_of, modes),
         out_shape=(
             shape(local.shape, F32),
-            shape((subs, 4 * wide + 8, width), F32),
+            shape((subs, 4 * wide, width), F32),
         ),
-        in_specs=[SMEM] + [VMEM] * 8,
+        in_specs=[SMEM] + [VMEM] * 9,
         out_specs=(VMEM, VMEM),
         compiler_params=params(),
         name="halo",
-    )(info, from_other, from_pair, flow_coupling, block, radial1, ends, axial, local)
+    )(info, from_other, from_pair, flow_coupling, block, radial1, ends, axial, mask, local)
     received = lax.all_to_all(message, "mer", 0, 0)
 
     system = np.diag(np.full(subs - 1, SCHUR_DIAG)) - np.eye(subs - 1, k=1) - np.eye(subs - 1, k=-1)
     w, sums = pl.pallas_call(
-        functools.partial(project_kernel, sub_of, np.linalg.inv(system)),
+        functools.partial(
+            project_kernel, sub_of, np.linalg.inv(system), float(width - iface_index.shape[0])
+        ),
         out_shape=(shape(local.shape, F32), shape((inner, 1, 128), F32)),
         in_specs=[SMEM] + [VMEM] * 6,
         out_specs=(VMEM, VMEM),

time: 62.6 us -> 62.3 us (level)
    all_to_all x1, blocking collectives: 9.49 us -> 8.83 us  [body(): received = lax.all_to_all(message, 'mer', 0, 0)]
where the time goes in v4:
time: 62.3 us; the launch traced here: 62 us
  blocking collectives  42 us (67%)
  starting transfers between devices  9.46 us (15%)
  Pallas kernels  9.06 us (15%)
  between operations  0.78 us (1%)
  local copies, waits for them, and re-layouts  0.72 us (1%)
    all_to_all x1, blocking collectives, body(): sums = lax.all_to_all(sums, 'inner', 0, 0)  16.9 us
    all_to_all x1, blocking collectives, body(): sums = lax.all_to_all(sums, ('outer', 'mer'), 0, 0)  16.2 us
    all_to_all x1, blocking collectives, body(): received = lax.all_to_all(message, 'mer', 0, 0)  8.83 us
    ppermute x1, starting transfers between devices, body(): from_other = lax.ppermute(to_other, mode, other)  5.4 us
    ppermute x1, starting transfers between devices, body(): from_pair = lax.ppermute(to_pair, mode, [(i, i ^ 1) for i in range(groups)])  4.07 us
    pallas_call x1, Pallas kernels, body(): pl.pallas_call(functools.partial(layout_kernel, group_of, krylov), out_sh...  2.42 us
    pallas_call x1, Pallas kernels, body(): pl.pallas_call(functools.partial(inner_kernel, modes), out_shape=(shape((...  2.41 us
    pallas_call x1, Pallas kernels, body(): pl.pallas_call(functools.partial(finish_kernel, float(modes * points * su...  1.88 us
  transfers between devices with their start and end apart: 2, of which 0 were waited for; matrix products, arithmetic and copies ran while one was open for 0% of the time, Pallas kernels for 4%

profile of v4, /device:TPU:1, one launch (start us, length us, event | category | flops | bytes accessed | tf_op | source)
XLA Modules:
  0.0 62.0 jit_solution(8865025970555091640)
XLA Ops:
  0.6 0.0 copy-start.5
  0.6 0.7 %copy-done.5 = s32[512]{0:T(512)S(1)} copy-done((s32[512]{0:T(512)S(1)}, s32[512]{0:T(512)}, u32[]{:S(2)}) %copy-start.5) | copy-done | bytes 2072
  1.3 0.0 copy-start
  1.3 0.0 copy-start.1
  1.3 0.0 copy-start.2
  1.3 0.0 copy-start.3
  1.3 0.0 copy-start.4
  1.3 0.0 copy-start.6
  1.3 0.0 copy-start.7
  1.4 2.4 %layout.1 = (s32[2]{0:T(128)S(1)}, f32[2,2,32,256]{3,2,1,0:T(8,128)S(1)}, f32[2,2,32,256]{3,2,1,0:T(8,128)S(1)}) custom-call(s32[4,128]{1,0:T(4,128)S(1)} %bitcast.3, f32[4,2,8,32,256]{4,3,2,1,0:T(8,128)} %basis_ref.7), custom_call_target="tpu_custom_call" | custom-call | flops 10000000000 | bytes 262144 | tf_op jit(solution)/shard_map/layout/pallas_call | solution.py:474
  3.8 5.4 %collective-permute-start = (f32[2,2,32,256]{3,2,1,0:T(8,128)S(1)}, f32[2,2,32,256]{3,2,1,0:T(8,128)S(1)}, u32[]{:S(2)}, u32[]{:S(2)}) collective-permute-start(f32[2,2,32,256]{3,2,1,0:T(8,128)S(1)} %get-tuple-element.20), channel_id=1, source_target_pairs={{4,8},{12,16},{20,24},{28,32},{36,40},{44,48},{52,56},{60,64},{68,... | collective-permute-start | bytes 393224 | tf_op jit(solution)/shard_map/ppermute | solution.py:490
  9.2 4.1 %collective-permute-start.1 = (f32[2,2,32,256]{3,2,1,0:T(8,128)S(1)}, f32[2,2,32,256]{3,2,1,0:T(8,128)S(1)}, u32[]{:S(2)}, u32[]{:S(2)}) collective-permute-start(f32[2,2,32,256]{3,2,1,0:T(8,128)S(1)} %get-tuple-element.21), channel_id=1, source_target_pairs={{0,4},{4,0},{8,12},{12,8},{16,20},{20,16},{24,28},{28,24},{32,36},... | collective-permute-start | bytes 393224 | tf_op jit(solution)/shard_map/ppermute | solution.py:491
  13.3 0.0 copy-done
  13.3 0.0 copy-done.1
  13.3 0.0 copy-done.2
  13.3 0.0 copy-done.3
  13.3 0.0 copy-done.4
  13.3 0.0 copy-done.6
  13.3 0.0 copy-done.7
  13.3 2.4 %inner.1 = (f32[2,8,32,256]{3,2,1,0:T(8,128)S(1)}, f32[2,16,256]{2,1,0:T(8,128)S(1)}, bf16[2,256,256]{2,1,0:T(8,128)(2,1)S(1)}, bf16[2,256,256]{2,1,0:T(8,128)(2...) custom-call(s32[2]{0:T(128)S(1)} %get-tuple-element.19.info_ref, s32[1,128]{1,0:T(1,128)S(1)} %bitcast.4, ...), custom_call_target="tpu_custom_call" | custom-call | flops 1000000000 | bytes 8388608 | tf_op jit(solution)/shard_map/inner/pallas_call | solution.py:494
  15.7 0.0 collective-permute-done.other_ref
  15.8 0.0 collective-permute-done.1.pair_ref
  15.8 1.2 %halo.1 = (f32[2,8,32,256]{3,2,1,0:T(8,128)S(1)}, f32[4,64,256]{2,1,0:T(8,128)S(1)}) custom-call(s32[2]{0:T(128)S(1)} %get-tuple-element.19.info_ref, f32[2,2,32,256]{3,2,1,0:T(8,128)S(1)} %collective-permute-done.other_ref, f32[2,2,32,256]{3,2,1,0:T(8,128)S(1)} %collective-permute-done.1.pair_ref, f32[4,32,256]{2,1,0:T(8,128)S(1)} %copy-done.2, ...), custom_call_target="tpu_custom_call" | custom-call | tf_op jit(solution)/shard_map/halo/pallas_call | solution.py:513
  17.0 8.8 %all_to_all.15.received_ref = f32[4,64,256]{2,1,0:T(8,128)S(1)} all-to-all(f32[4,64,256]{2,1,0:T(8,128)S(1)} %get-tuple-element.27), channel_id=1, replica_groups=mesh['outer'=8,'inner'=16,'mer'=4] {'mer'}, dimensions={0} | all-to-all | bytes 524288 | tf_op jit(solution)/shard_map/all_to_all | solution.py:524
  25.8 1.2 %project.1 = (f32[2,8,32,256]{3,2,1,0:T(8,128)S(1)}, f32[16,1,128]{2,1,0:T(1,128)S(1)}) custom-call(s32[2]{0:T(128)S(1)} %get-tuple-element.19.info_ref, f32[4,64,256]{2,1,0:T(8,128)S(1)} %all_to_all.15.received_ref, f32[1,256]{1,0:T(1,128)S(1)} %get-tuple-element.25.mask_ref, f32[2,32,32]{2,1,0:T(8,128)S(1)} %copy-done.1, ...), custom_call_target="tpu_custom_call" | custom-call | tf_op jit(solution)/shard_map/project/pallas_call | solution.py:527
  27.0 16.9 %all_to_all.16 = f32[16,1,128]{2,1,0:T(1,128)S(1)} all-to-all(f32[16,1,128]{2,1,0:T(1,128)S(1)} %get-tuple-element.30), channel_id=1, replica_groups=mesh['outer'=8,'inner'=16,'mer'=4] {'inner'}, dimensions={0} | all-to-all | bytes 16384 | tf_op jit(solution)/shard_map/all_to_all | solution.py:539
  43.9 16.2 %all_to_all.17.sums_ref = f32[32,1,128]{2,1,0:T(1,128)S(1)} all-to-all(f32[32,1,128]{2,1,0:T(1,128)S(1)} %broadcast_in_dim.2), channel_id=1, replica_groups=mesh['outer'=8,'inner'=16,'mer'=4] {'outer','mer'}, dimensions={0} | all-to-all | bytes 32768 | tf_op jit(solution)/shard_map/all_to_all | solution.py:541
  60.1 1.9 %finish.1 = (f32[2,8,32,256]{3,2,1,0:T(8,128)}, f32[2,4]{1,0:T(2,128)}, f32[1,1]{1,0:T(1,128)}) custom-call(s32[2]{0:T(128)S(1)} %get-tuple-element.19.info_ref, f32[32,1,128]{2,1,0:T(1,128)S(1)} %all_to_all.17.sums_ref, f32[4,2,8,32,256]{4,3,2,1,0:T(8,128)S(1)} %copy-done, f32[2,8,32,256]{3,2,1,0:T(8,128)S(1)} %get-tuple-element.31.w_ref), custom_call_target="tpu_custom_call" | custom-call | tf_op jit(solution)/shard_map/finish/pallas_call | solution.py:543
  (2 shorter events, 0.0 us)
Async XLA Ops:
  0.6 0.7 %copy-start.5 = (s32[512]{0:T(512)S(1)}, s32[512]{0:T(512)}, u32[]{:S(2)}) copy-start(s32[512]{0:T(512)} %param.8) | copy-start | bytes 6148
  1.3 11.9 %copy-start = (f32[4,2,8,32,256]{4,3,2,1,0:T(8,128)S(1)}, f32[4,2,8,32,256]{4,3,2,1,0:T(8,128)}, u32[]{:S(2)}) copy-start(f32[4,2,8,32,256]{4,3,2,1,0:T(8,128)} %basis_ref.7) | copy-start | bytes 6291460
  1.3 12.0 %copy-start.1 = (f32[2,32,32]{2,1,0:T(8,128)S(1)}, f32[2,32,32]{2,1,0:T(8,128)}, u32[]{:S(2)}) copy-start(f32[2,32,32]{2,1,0:T(8,128)} %axial_ref.5) | copy-start | bytes 24580
  1.3 12.0 %copy-start.2 = (f32[4,32,256]{2,1,0:T(8,128)S(1)}, f32[4,32,256]{2,1,0:T(8,128)}, u32[]{:S(2)}) copy-start(f32[4,32,256]{2,1,0:T(8,128)} %flow_ref.3) | copy-start | bytes 393220
  1.3 12.0 %copy-start.3 = (f32[2,256,256]{2,1,0:T(8,128)S(1)}, f32[2,256,256]{2,1,0:T(8,128)}, u32[]{:S(2)}) copy-start(f32[2,256,256]{2,1,0:T(8,128)} %radial_ref.1) | copy-start | bytes 1572868
  1.3 12.0 %copy-start.4 = (f32[32,256]{1,0:T(8,128)S(1)}, f32[32,256]{1,0:T(8,128)}, u32[]{:S(2)}) copy-start(f32[32,256]{1,0:T(8,128)} %swirl_ref.1) | copy-start | bytes 98308
  1.3 12.0 %copy-start.6 = (s32[128]{0:T(128)S(1)}, s32[128]{0:T(128)}, u32[]{:S(2)}) copy-start(s32[128]{0:T(128)} %param.9) | copy-start | bytes 1540
  1.3 12.0 %copy-start.7 = (f32[2]{0:T(128)S(1)}, f32[2]{0:T(128)}, u32[]{:S(2)}) copy-start(f32[2]{0:T(128)} %shift_ref.1) | copy-start | bytes 28
  3.8 12.0 %collective-permute-start = (f32[2,2,32,256]{3,2,1,0:T(8,128)S(1)}, f32[2,2,32,256]{3,2,1,0:T(8,128)S(1)}, u32[]{:S(2)}, u32[]{:S(2)}) collective-permute-start(f32[2,2,32,256]{3,2,1,0:T(8,128)S(1)} %get-tuple-element.20), channel_id=1, source_target_pairs={{4,8},{12,16},{20,24},{28,32},{36,40},{44,48},{52,56},{60,64},{68,... | collective-permute-start | bytes 393224 | tf_op jit(solution)/shard_map/ppermute | solution.py:490
  9.2 6.6 %collective-permute-start.1 = (f32[2,2,32,256]{3,2,1,0:T(8,128)S(1)}, f32[2,2,32,256]{3,2,1,0:T(8,128)S(1)}, u32[]{:S(2)}, u32[]{:S(2)}) collective-permute-start(f32[2,2,32,256]{3,2,1,0:T(8,128)S(1)} %get-tuple-element.21), channel_id=1, source_target_pairs={{0,4},{4,0},{8,12},{12,8},{16,20},{20,16},{24,28},{28,24},{32,36},... | collective-permute-start | bytes 393224 | tf_op jit(solution)/shard_map/ppermute | solution.py:491

commit v5 on v4

--- a/solution.py
+++ b/solution.py
@@ -482,7 +482,7 @@
         out_specs=(SMEM, VMEM, VMEM),
         scratch_shapes=[pltpu.SemaphoreType.DMA((2, 2))],
         compiler_params=params(52),
-        cost_estimate=pl.CostEstimate(flops=10**10, bytes_accessed=2**18, transcendentals=0),
+        cost_estimate=pl.CostEstimate(flops=10**9, bytes_accessed=2**18, transcendentals=0),
         name="layout",
     )(mode_cost.reshape(-1, math.gcd(modes, 128)), basis)
     other = [(i, i + 1) for i in range(1, groups - 1, 2)]

time: 62.3 us -> 62.4 us (level)
  no operation moved by 1% of the time
where the time goes in v5:
time: 62.4 us; the launch traced here: 62.1 us
  blocking collectives  42.3 us (68%)
  starting transfers between devices  9.45 us (15%)
  Pallas kernels  8.63 us (14%)
  local copies, waits for them, and re-layouts  0.87 us (1%)
  between operations  0.79 us (1%)
    all_to_all x1, blocking collectives, body(): sums = lax.all_to_all(sums, 'inner', 0, 0)  17.3 us
    all_to_all x1, blocking collectives, body(): sums = lax.all_to_all(sums, ('outer', 'mer'), 0, 0)  16.2 us
    all_to_all x1, blocking collectives, body(): received = lax.all_to_all(message, 'mer', 0, 0)  8.82 us
    ppermute x1, starting transfers between devices, body(): from_other = lax.ppermute(to_other, mode, other)  5.39 us
    ppermute x1, starting transfers between devices, body(): from_pair = lax.ppermute(to_pair, mode, [(i, i ^ 1) for i in range(groups)])  4.07 us
    pallas_call x1, Pallas kernels, body(): pl.pallas_call(functools.partial(inner_kernel, modes), out_shape=(shape((...  2.33 us
    pallas_call x1, Pallas kernels, body(): pl.pallas_call(functools.partial(layout_kernel, group_of, krylov), out_sh...  2.23 us
    pallas_call x1, Pallas kernels, body(): pl.pallas_call(functools.partial(finish_kernel, float(modes * points * su...  1.84 us
  transfers between devices with their start and end apart: 2, of which 0 were waited for; matrix products, arithmetic and copies ran while one was open for 0% of the time, Pallas kernels for 4%

profile of v5, /device:TPU:1, one launch (start us, length us, event | category | flops | bytes accessed | tf_op | source)
XLA Modules:
  0.0 62.1 jit_solution(13392371233500809572)
XLA Ops:
  0.6 0.0 copy-start
  0.6 0.0 copy-start.1
  0.7 0.0 copy-start.2
  0.7 0.0 copy-start.4
  0.7 0.0 copy-start.3
  0.7 0.0 copy-start.5
  0.7 0.8 %copy-done.5 = s32[512]{0:T(512)S(1)} copy-done((s32[512]{0:T(512)S(1)}, s32[512]{0:T(512)}, u32[]{:S(2)}) %copy-start.5) | copy-done | bytes 2072
  1.5 0.0 copy-start.6
  1.5 0.0 copy-start.7
  1.5 2.2 %layout.1 = (s32[2]{0:T(128)S(1)}, f32[2,2,32,256]{3,2,1,0:T(8,128)S(1)}, f32[2,2,32,256]{3,2,1,0:T(8,128)S(1)}) custom-call(s32[4,128]{1,0:T(4,128)S(1)} %bitcast.3, f32[4,2,8,32,256]{4,3,2,1,0:T(8,128)} %basis_ref.7), custom_call_target="tpu_custom_call" | custom-call | flops 1000000000 | bytes 262144 | tf_op jit(solution)/shard_map/layout/pallas_call | solution.py:474
  3.8 5.4 %collective-permute-start = (f32[2,2,32,256]{3,2,1,0:T(8,128)S(1)}, f32[2,2,32,256]{3,2,1,0:T(8,128)S(1)}, u32[]{:S(2)}, u32[]{:S(2)}) collective-permute-start(f32[2,2,32,256]{3,2,1,0:T(8,128)S(1)} %get-tuple-element.20), channel_id=1, source_target_pairs={{4,8},{12,16},{20,24},{28,32},{36,40},{44,48},{52,56},{60,64},{68,... | collective-permute-start | bytes 393224 | tf_op jit(solution)/shard_map/ppermute | solution.py:490
  9.2 4.1 %collective-permute-start.1 = (f32[2,2,32,256]{3,2,1,0:T(8,128)S(1)}, f32[2,2,32,256]{3,2,1,0:T(8,128)S(1)}, u32[]{:S(2)}, u32[]{:S(2)}) collective-permute-start(f32[2,2,32,256]{3,2,1,0:T(8,128)S(1)} %get-tuple-element.21), channel_id=1, source_target_pairs={{0,4},{4,0},{8,12},{12,8},{16,20},{20,16},{24,28},{28,24},{32,36},... | collective-permute-start | bytes 393224 | tf_op jit(solution)/shard_map/ppermute | solution.py:491
  13.2 0.0 copy-done
  13.2 0.0 copy-done.1
  13.2 0.0 copy-done.2
  13.3 0.0 copy-done.4
  13.3 0.0 copy-done.3
  13.3 0.0 copy-done.6
  13.3 0.0 copy-done.7
  13.3 2.3 %inner.1 = (f32[2,8,32,256]{3,2,1,0:T(8,128)S(1)}, f32[2,16,256]{2,1,0:T(8,128)S(1)}, bf16[2,256,256]{2,1,0:T(8,128)(2,1)S(1)}, bf16[2,256,256]{2,1,0:T(8,128)(2...) custom-call(s32[2]{0:T(128)S(1)} %get-tuple-element.19.info_ref, s32[1,128]{1,0:T(1,128)S(1)} %bitcast.4, ...), custom_call_target="tpu_custom_call" | custom-call | flops 1000000000 | bytes 8388608 | tf_op jit(solution)/shard_map/inner/pallas_call | solution.py:494
  15.6 0.0 collective-permute-done.other_ref
  15.6 0.0 collective-permute-done.1.pair_ref
  15.7 1.2 %halo.1 = (f32[2,8,32,256]{3,2,1,0:T(8,128)S(1)}, f32[4,64,256]{2,1,0:T(8,128)S(1)}) custom-call(s32[2]{0:T(128)S(1)} %get-tuple-element.19.info_ref, f32[2,2,32,256]{3,2,1,0:T(8,128)S(1)} %collective-permute-done.other_ref, f32[2,2,32,256]{3,2,1,0:T(8,128)S(1)} %collective-permute-done.1.pair_ref, f32[4,32,256]{2,1,0:T(8,128)S(1)} %copy-done.2, ...), custom_call_target="tpu_custom_call" | custom-call | tf_op jit(solution)/shard_map/halo/pallas_call | solution.py:513
  16.9 8.8 %all_to_all.15.received_ref = f32[4,64,256]{2,1,0:T(8,128)S(1)} all-to-all(f32[4,64,256]{2,1,0:T(8,128)S(1)} %get-tuple-element.27), channel_id=1, replica_groups=mesh['outer'=8,'inner'=16,'mer'=4] {'mer'}, dimensions={0} | all-to-all | bytes 524288 | tf_op jit(solution)/shard_map/all_to_all | solution.py:524
  25.7 1.0 %project.1 = (f32[2,8,32,256]{3,2,1,0:T(8,128)S(1)}, f32[16,1,128]{2,1,0:T(1,128)S(1)}) custom-call(s32[2]{0:T(128)S(1)} %get-tuple-element.19.info_ref, f32[4,64,256]{2,1,0:T(8,128)S(1)} %all_to_all.15.received_ref, f32[1,256]{1,0:T(1,128)S(1)} %get-tuple-element.25.mask_ref, f32[2,32,32]{2,1,0:T(8,128)S(1)} %copy-done.1, ...), custom_call_target="tpu_custom_call" | custom-call | tf_op jit(solution)/shard_map/project/pallas_call | solution.py:527
  26.7 17.3 %all_to_all.16 = f32[16,1,128]{2,1,0:T(1,128)S(1)} all-to-all(f32[16,1,128]{2,1,0:T(1,128)S(1)} %get-tuple-element.30), channel_id=1, replica_groups=mesh['outer'=8,'inner'=16,'mer'=4] {'inner'}, dimensions={0} | all-to-all | bytes 16384 | tf_op jit(solution)/shard_map/all_to_all | solution.py:539
  44.1 16.2 %all_to_all.17.sums_ref = f32[32,1,128]{2,1,0:T(1,128)S(1)} all-to-all(f32[32,1,128]{2,1,0:T(1,128)S(1)} %broadcast_in_dim.2), channel_id=1, replica_groups=mesh['outer'=8,'inner'=16,'mer'=4] {'outer','mer'}, dimensions={0} | all-to-all | bytes 32768 | tf_op jit(solution)/shard_map/all_to_all | solution.py:541
  60.3 1.8 %finish.1 = (f32[2,8,32,256]{3,2,1,0:T(8,128)}, f32[2,4]{1,0:T(2,128)}, f32[1,1]{1,0:T(1,128)}) custom-call(s32[2]{0:T(128)S(1)} %get-tuple-element.19.info_ref, f32[32,1,128]{2,1,0:T(1,128)S(1)} %all_to_all.17.sums_ref, f32[4,2,8,32,256]{4,3,2,1,0:T(8,128)S(1)} %copy-done, f32[2,8,32,256]{3,2,1,0:T(8,128)S(1)} %get-tuple-element.31.w_ref), custom_call_target="tpu_custom_call" | custom-call | tf_op jit(solution)/shard_map/finish/pallas_call | solution.py:543
  (2 shorter events, 0.0 us)
Async XLA Ops:
  0.6 12.6 %copy-start = (f32[4,2,8,32,256]{4,3,2,1,0:T(8,128)S(1)}, f32[4,2,8,32,256]{4,3,2,1,0:T(8,128)}, u32[]{:S(2)}) copy-start(f32[4,2,8,32,256]{4,3,2,1,0:T(8,128)} %basis_ref.7) | copy-start | bytes 6291460
  0.6 12.6 %copy-start.1 = (f32[2,32,32]{2,1,0:T(8,128)S(1)}, f32[2,32,32]{2,1,0:T(8,128)}, u32[]{:S(2)}) copy-start(f32[2,32,32]{2,1,0:T(8,128)} %axial_ref.5) | copy-start | bytes 24580
  0.7 12.6 %copy-start.2 = (f32[4,32,256]{2,1,0:T(8,128)S(1)}, f32[4,32,256]{2,1,0:T(8,128)}, u32[]{:S(2)}) copy-start(f32[4,32,256]{2,1,0:T(8,128)} %flow_ref.3) | copy-start | bytes 393220
  0.7 12.6 %copy-start.4 = (f32[32,256]{1,0:T(8,128)S(1)}, f32[32,256]{1,0:T(8,128)}, u32[]{:S(2)}) copy-start(f32[32,256]{1,0:T(8,128)} %swirl_ref.1) | copy-start | bytes 98308
  0.7 12.6 %copy-start.3 = (f32[2,256,256]{2,1,0:T(8,128)S(1)}, f32[2,256,256]{2,1,0:T(8,128)}, u32[]{:S(2)}) copy-start(f32[2,256,256]{2,1,0:T(8,128)} %radial_ref.1) | copy-start | bytes 1572868
  0.7 0.8 %copy-start.5 = (s32[512]{0:T(512)S(1)}, s32[512]{0:T(512)}, u32[]{:S(2)}) copy-start(s32[512]{0:T(512)} %param.8) | copy-start | bytes 6148
  1.5 11.8 %copy-start.6 = (s32[128]{0:T(128)S(1)}, s32[128]{0:T(128)}, u32[]{:S(2)}) copy-start(s32[128]{0:T(128)} %param.9) | copy-start | bytes 1540
  1.5 11.8 %copy-start.7 = (f32[2]{0:T(128)S(1)}, f32[2]{0:T(128)}, u32[]{:S(2)}) copy-start(f32[2]{0:T(128)} %shift_ref.1) | copy-start | bytes 28
  3.8 11.9 %collective-permute-start = (f32[2,2,32,256]{3,2,1,0:T(8,128)S(1)}, f32[2,2,32,256]{3,2,1,0:T(8,128)S(1)}, u32[]{:S(2)}, u32[]{:S(2)}) collective-permute-start(f32[2,2,32,256]{3,2,1,0:T(8,128)S(1)} %get-tuple-element.20), channel_id=1, source_target_pairs={{4,8},{12,16},{20,24},{28,32},{36,40},{44,48},{52,56},{60,64},{68,... | collective-permute-start | bytes 393224 | tf_op jit(solution)/shard_map/ppermute | solution.py:490
  9.2 6.5 %collective-permute-start.1 = (f32[2,2,32,256]{3,2,1,0:T(8,128)S(1)}, f32[2,2,32,256]{3,2,1,0:T(8,128)S(1)}, u32[]{:S(2)}, u32[]{:S(2)}) collective-permute-start(f32[2,2,32,256]{3,2,1,0:T(8,128)S(1)} %get-tuple-element.21), channel_id=1, source_target_pairs={{0,4},{4,0},{8,12},{12,8},{16,20},{20,16},{24,28},{28,24},{32,36},... | collective-permute-start | bytes 393224 | tf_op jit(solution)/shard_map/ppermute | solution.py:491
